TPU v7x, 32 devices: a whole 2x2x4 slice. The times are simulated.
32 devices in a mesh: seq: 2 (over x), shard: 16 (over z, y, core).
Axes of the slice: x: 2, y: 2, z: 4, core: 2. Of those that a mesh axis runs over, the one named last changes fastest.
Arguments:
- tokens: bfloat16 [16, 320, 2048], P('shard', 'seq'), may hold values from -6 to 6
- cotangent: bfloat16 [16, 320, 2048], P('shard', 'seq'), may hold values from -6 to 6
- norm1_gain: bfloat16 [2048], P(('seq', 'shard')), may hold values from 0.25 to 1.75
- norm1_bias: bfloat16 [2048], P(('seq', 'shard')), may hold values from -3 to 3
- qkv_weight: bfloat16 [2048, 6144], P(('seq', 'shard')), may hold values from -0.125 to 0.125
- qkv_bias: bfloat16 [6144], P(('seq', 'shard')), may hold values from -3 to 3
- out_weight: bfloat16 [2048, 2048], P(('seq', 'shard')), may hold values from -0.5 to 0.5
- norm2_gain: bfloat16 [2048], P(('seq', 'shard')), may hold values from 0.25 to 1.75
- norm2_bias: bfloat16 [2048], P(('seq', 'shard')), may hold values from -3 to 3
- gate_weight: bfloat16 [2048, 5632], P(('seq', 'shard')), may hold values from -0.125 to 0.125
- up_weight: bfloat16 [2048, 5632], P(('seq', 'shard')), may hold values from -0.125 to 0.125
- down_weight: bfloat16 [5632, 2048], P(('seq', 'shard')), may hold values from -0.078125 to 0.078125
Outputs:
- out: bfloat16 [16, 320, 2048], P('shard', 'seq')
- d_input: float32 [16, 320, 2048], P('shard', 'seq')
- norm1_gain_grad: float32 [2048], P(('seq', 'shard'))
- norm1_bias_grad: float32 [2048], P(('seq', 'shard'))
- qkv_weight_grad: float32 [2048, 6144], P(('seq', 'shard'))
- qkv_bias_grad: float32 [6144], P(('seq', 'shard'))
- out_weight_grad: float32 [2048, 2048], P(('seq', 'shard'))
- norm2_gain_grad: float32 [2048], P(('seq', 'shard'))
- norm2_bias_grad: float32 [2048], P(('seq', 'shard'))
- gate_weight_grad: float32 [2048, 5632], P(('seq', 'shard'))
- up_weight_grad: float32 [2048, 5632], P(('seq', 'shard'))
- down_weight_grad: float32 [5632, 2048], P(('seq', 'shard'))
All inputs are finite; a program needn't handle non-finite values.
Results may differ from a plain program's by a relative error of at most 0.012.
Values may be sent and summed in bfloat16 or wider, within the bound.
A program may use at most 448 MiB of HBM per device.

v0:
```python
import jax
import jax.numpy as jnp
from jax import lax
from jax.sharding import PartitionSpec as P

HEADS = 32
HEAD_DIM = 64
ROTARY = 16


def norm_rows(values):
    centre = jnp.mean(values, axis=-1, keepdims=True)
    centred = values - centre
    spread = jnp.mean(centred * centred, axis=-1, keepdims=True)
    scale_rows = lax.rsqrt(spread + 1e-05)
    return (centred * scale_rows, scale_rows)


def norm_back(grad_normed, normed, scale_rows):
    return scale_rows * (
        grad_normed
        - jnp.mean(grad_normed, axis=-1, keepdims=True)
        - normed * jnp.mean(grad_normed * normed, axis=-1, keepdims=True)
    )


def rotate(values, positions, direction):
    halves = ROTARY // 2
    frequency = 10000.0 ** (-2.0 * jnp.arange(halves, dtype=jnp.float32) / ROTARY)
    angles = positions.astype(jnp.float32)[:, None] * frequency[None, :]
    cosine_table = jnp.cos(angles)[:, None, :]
    sine_table = jnp.sin(angles)[:, None, :] * direction
    first_half = values[..., :halves]
    second_half = values[..., halves:ROTARY]
    return jnp.concatenate(
        [
            first_half * cosine_table - second_half * sine_table,
            second_half * cosine_table + first_half * sine_table,
            values[..., ROTARY:],
        ],
        axis=-1,
    )


def to_heads(values, groups):
    return values.reshape(values.shape[0], groups, values.shape[1] // groups)


def split_heads(values):
    return values.reshape(values.shape[0], values.shape[2] // HEAD_DIM, HEAD_DIM).transpose(1, 0, 2)


def join_heads(values):
    return values.transpose(1, 0, 2).reshape(values.shape[1], 1, values.shape[0] * HEAD_DIM)


def causal_scores(query_block, key_block):
    scores = (
        jnp.einsum("qd,kd->qk", query_block, key_block, preferred_element_type=jnp.float32) * 0.125
    )
    rows_index = lax.broadcasted_iota(jnp.int32, scores.shape, 0)
    cols_index = lax.broadcasted_iota(jnp.int32, scores.shape, 1)
    return jnp.where(rows_index >= cols_index, scores, -1e30)


def attend(inputs):
    query_block, key_block, value_block = inputs
    scores = causal_scores(query_block, key_block)
    highest = jnp.max(scores, axis=-1, keepdims=True)
    exponent = jnp.exp(scores - highest)
    totals = jnp.sum(exponent, axis=-1, keepdims=True)
    weights = (exponent / totals).astype(jnp.bfloat16)
    mixed = jnp.dot(weights, value_block, preferred_element_type=jnp.float32).astype(jnp.bfloat16)
    return (mixed, (highest + jnp.log(totals))[:, 0])


def attend_back(inputs):
    query_block, key_block, value_block, grad_block, log_totals = inputs
    scores = causal_scores(query_block, key_block)
    weights = jnp.exp(scores - log_totals[:, None])
    grad_weights = jnp.einsum(
        "qd,kd->qk", grad_block, value_block, preferred_element_type=jnp.float32
    )
    grad_scores = (
        weights * (grad_weights - jnp.sum(weights * grad_weights, axis=-1, keepdims=True))
    ).astype(jnp.bfloat16)
    grad_query = (
        jnp.dot(grad_scores, key_block, preferred_element_type=jnp.float32) * 0.125
    ).astype(jnp.bfloat16)
    grad_key = (
        jnp.einsum("qk,qd->kd", grad_scores, query_block, preferred_element_type=jnp.float32)
        * 0.125
    ).astype(jnp.bfloat16)
    grad_value = jnp.einsum(
        "qk,qd->kd", weights.astype(jnp.bfloat16), grad_block, preferred_element_type=jnp.float32
    ).astype(jnp.bfloat16)
    return (grad_query, grad_key, grad_value)


def per_device(
    tokens,
    cotangent,
    norm1_gain,
    norm1_bias,
    qkv_weight,
    qkv_bias,
    out_weight,
    norm2_gain,
    norm2_bias,
    gate_weight,
    up_weight,
    down_weight,
):
    groups = lax.axis_size("seq")
    row_count = tokens.shape[1]
    model_width = tokens.shape[2]
    inputs = tokens[0].astype(jnp.float32)
    positions = lax.axis_index("seq") * row_count + jnp.arange(row_count, dtype=jnp.int32)
    first_gain, first_bias, qkv_matrix, qkv_offset, out_matrix = (
        lax.all_gather(norm1_gain, ("seq", "shard"), axis=0, tiled=True),
        lax.all_gather(norm1_bias, ("seq", "shard"), axis=0, tiled=True),
        lax.all_gather(qkv_weight, ("seq", "shard"), axis=0, tiled=True),
        lax.all_gather(qkv_bias, ("seq", "shard"), axis=0, tiled=True),
        lax.all_gather(out_weight, ("seq", "shard"), axis=0, tiled=True),
    )
    first_normed, first_scale = norm_rows(inputs)
    first_input = (
        first_normed * first_gain.astype(jnp.float32) + first_bias.astype(jnp.float32)
    ).astype(jnp.bfloat16)
    projected = jnp.dot(
        first_input, qkv_matrix, preferred_element_type=jnp.float32
    ) + qkv_offset.astype(jnp.float32)
    query_tok = rotate(
        projected[:, :model_width].reshape(row_count, HEADS, HEAD_DIM), positions, 1.0
    )
    key_tok = rotate(
        projected[:, model_width : 2 * model_width].reshape(row_count, HEADS, HEAD_DIM),
        positions,
        1.0,
    )
    query_tok = query_tok.reshape(row_count, model_width).astype(jnp.bfloat16)
    key_tok = key_tok.reshape(row_count, model_width).astype(jnp.bfloat16)
    value_tok = projected[:, 2 * model_width :].astype(jnp.bfloat16)
    query_heads, key_heads, value_heads = (
        lax.all_to_all(to_heads(query_tok, groups), "seq", split_axis=1, concat_axis=0, tiled=True),
        lax.all_to_all(to_heads(key_tok, groups), "seq", split_axis=1, concat_axis=0, tiled=True),
        lax.all_to_all(to_heads(value_tok, groups), "seq", split_axis=1, concat_axis=0, tiled=True),
    )
    query_split = split_heads(query_heads)
    key_split = split_heads(key_heads)
    value_split = split_heads(value_heads)
    mixed_heads, log_totals = lax.map(attend, (query_split, key_split, value_split))
    mixed_tok = lax.all_to_all(
        join_heads(mixed_heads), "seq", split_axis=0, concat_axis=1, tiled=True
    ).reshape(row_count, model_width)
    middle = inputs + jnp.dot(mixed_tok, out_matrix, preferred_element_type=jnp.float32)
    second_gain, second_bias, gate_matrix, up_matrix, down_matrix = (
        lax.all_gather(norm2_gain, ("seq", "shard"), axis=0, tiled=True),
        lax.all_gather(norm2_bias, ("seq", "shard"), axis=0, tiled=True),
        lax.all_gather(gate_weight, ("seq", "shard"), axis=0, tiled=True),
        lax.all_gather(up_weight, ("seq", "shard"), axis=0, tiled=True),
        lax.all_gather(down_weight, ("seq", "shard"), axis=0, tiled=True),
    )
    second_normed, second_scale = norm_rows(middle)
    second_input = (
        second_normed * second_gain.astype(jnp.float32) + second_bias.astype(jnp.float32)
    ).astype(jnp.bfloat16)
    gate_rows = jnp.dot(second_input, gate_matrix, preferred_element_type=jnp.float32)
    up_rows = jnp.dot(second_input, up_matrix, preferred_element_type=jnp.float32)
    sigmoid_gate = jax.nn.sigmoid(gate_rows)
    silu_gate = gate_rows * sigmoid_gate
    hidden = (silu_gate * up_rows).astype(jnp.bfloat16)
    result = middle + jnp.dot(hidden, down_matrix, preferred_element_type=jnp.float32)
    upstream = cotangent[0]
    second_gain, second_bias, gate_matrix, up_matrix, down_matrix = (
        lax.all_gather(norm2_gain, ("seq", "shard"), axis=0, tiled=True),
        lax.all_gather(norm2_bias, ("seq", "shard"), axis=0, tiled=True),
        lax.all_gather(gate_weight, ("seq", "shard"), axis=0, tiled=True),
        lax.all_gather(up_weight, ("seq", "shard"), axis=0, tiled=True),
        lax.all_gather(down_weight, ("seq", "shard"), axis=0, tiled=True),
    )
    grad_down_weight = jnp.einsum("tf,td->fd", hidden, upstream, preferred_element_type=jnp.float32)
    down_total = lax.psum_scatter(
        grad_down_weight, ("seq", "shard"), scatter_dimension=0, tiled=True
    )
    grad_hidden = jnp.einsum("td,fd->tf", upstream, down_matrix, preferred_element_type=jnp.float32)
    grad_gate = (
        grad_hidden * up_rows * sigmoid_gate * (1.0 + gate_rows * (1.0 - sigmoid_gate))
    ).astype(jnp.bfloat16)
    grad_up = (grad_hidden * silu_gate).astype(jnp.bfloat16)
    grad_gate_weight = jnp.einsum(
        "td,tf->df", second_input, grad_gate, preferred_element_type=jnp.float32
    )
    grad_up_weight = jnp.einsum(
        "td,tf->df", second_input, grad_up, preferred_element_type=jnp.float32
    )
    grad_second = jnp.einsum(
        "tf,df->td", grad_gate, gate_matrix, preferred_element_type=jnp.float32
    ) + jnp.einsum("tf,df->td", grad_up, up_matrix, preferred_element_type=jnp.float32)
    grad_second_gain = jnp.sum(grad_second * second_normed, axis=0)
    grad_second_bias = jnp.sum(grad_second, axis=0)
    grad_middle = upstream.astype(jnp.float32) + norm_back(
        grad_second * second_gain.astype(jnp.float32), second_normed, second_scale
    )
    mlp_totals = (
        lax.psum_scatter(grad_second_gain, ("seq", "shard"), scatter_dimension=0, tiled=True),
        lax.psum_scatter(grad_second_bias, ("seq", "shard"), scatter_dimension=0, tiled=True),
        lax.psum_scatter(grad_gate_weight, ("seq", "shard"), scatter_dimension=0, tiled=True),
        lax.psum_scatter(grad_up_weight, ("seq", "shard"), scatter_dimension=0, tiled=True),
    )
    first_gain, first_bias, qkv_matrix, qkv_offset, out_matrix = (
        lax.all_gather(norm1_gain, ("seq", "shard"), axis=0, tiled=True),
        lax.all_gather(norm1_bias, ("seq", "shard"), axis=0, tiled=True),
        lax.all_gather(qkv_weight, ("seq", "shard"), axis=0, tiled=True),
        lax.all_gather(qkv_bias, ("seq", "shard"), axis=0, tiled=True),
        lax.all_gather(out_weight, ("seq", "shard"), axis=0, tiled=True),
    )
    grad_attended = grad_middle.astype(jnp.bfloat16)
    grad_out_weight = jnp.einsum(
        "tc,td->cd", mixed_tok, grad_attended, preferred_element_type=jnp.float32
    )
    out_total = lax.psum_scatter(grad_out_weight, ("seq", "shard"), scatter_dimension=0, tiled=True)
    grad_mixed = jnp.einsum(
        "td,cd->tc", grad_attended, out_matrix, preferred_element_type=jnp.float32
    ).astype(jnp.bfloat16)
    grad_heads = lax.all_to_all(
        to_heads(grad_mixed, groups), "seq", split_axis=1, concat_axis=0, tiled=True
    )
    grad_query, grad_key, grad_value = lax.map(
        attend_back, (query_split, key_split, value_split, split_heads(grad_heads), log_totals)
    )
    query_back, key_back, value_back = (
        lax.all_to_all(join_heads(grad_query), "seq", split_axis=0, concat_axis=1, tiled=True),
        lax.all_to_all(join_heads(grad_key), "seq", split_axis=0, concat_axis=1, tiled=True),
        lax.all_to_all(join_heads(grad_value), "seq", split_axis=0, concat_axis=1, tiled=True),
    )
    grad_query_tok = rotate(
        query_back.reshape(row_count, HEADS, HEAD_DIM).astype(jnp.float32), positions, -1.0
    )
    grad_key_tok = rotate(
        key_back.reshape(row_count, HEADS, HEAD_DIM).astype(jnp.float32), positions, -1.0
    )
    grad_projected = jnp.concatenate(
        [
            grad_query_tok.reshape(row_count, model_width).astype(jnp.bfloat16),
            grad_key_tok.reshape(row_count, model_width).astype(jnp.bfloat16),
            value_back.reshape(row_count, model_width),
        ],
        axis=1,
    )
    grad_qkv_weight = jnp.einsum(
        "tc,te->ce", first_input, grad_projected, preferred_element_type=jnp.float32
    )
    grad_qkv_bias = jnp.sum(grad_projected.astype(jnp.float32), axis=0)
    grad_first = jnp.einsum(
        "te,ce->tc", grad_projected, qkv_matrix, preferred_element_type=jnp.float32
    )
    grad_first_gain = jnp.sum(grad_first * first_normed, axis=0)
    grad_first_bias = jnp.sum(grad_first, axis=0)
    grad_inputs = grad_middle + norm_back(
        grad_first * first_gain.astype(jnp.float32), first_normed, first_scale
    )
    attn_totals = (
        lax.psum_scatter(grad_first_gain, ("seq", "shard"), scatter_dimension=0, tiled=True),
        lax.psum_scatter(grad_first_bias, ("seq", "shard"), scatter_dimension=0, tiled=True),
        lax.psum_scatter(grad_qkv_weight, ("seq", "shard"), scatter_dimension=0, tiled=True),
        lax.psum_scatter(grad_qkv_bias, ("seq", "shard"), scatter_dimension=0, tiled=True),
    )
    return (
        result.astype(jnp.bfloat16)[None],
        grad_inputs[None],
        attn_totals[0],
        attn_totals[1],
        attn_totals[2],
        attn_totals[3],
        out_total,
        mlp_totals[0],
        mlp_totals[1],
        mlp_totals[2],
        mlp_totals[3],
        down_total,
    )


def solution(mesh):
    placed = (
        P("shard", "seq", None),
        P("shard", "seq", None),
        P(("seq", "shard")),
        P(("seq", "shard")),
        P(("seq", "shard"), None),
        P(("seq", "shard")),
        P(("seq", "shard"), None),
        P(("seq", "shard")),
        P(("seq", "shard")),
        P(("seq", "shard"), None),
        P(("seq", "shard"), None),
        P(("seq", "shard"), None),
    )
    return jax.shard_map(
        per_device,
        mesh=mesh,
        in_specs=placed,
        out_specs=(
            P("shard", "seq", None),
            P("shard", "seq", None),
            P(("seq", "shard")),
            P(("seq", "shard")),
            P(("seq", "shard"), None),
            P(("seq", "shard")),
            P(("seq", "shard"), None),
            P(("seq", "shard")),
            P(("seq", "shard")),
            P(("seq", "shard"), None),
            P(("seq", "shard"), None),
            P(("seq", "shard"), None),
        ),
        check_vma=False,
    )
```

profile of v0, /device:TPU:0, one launch (start us, length us, event | category | flops | bytes accessed | tf_op | source)
XLA Modules:
  0.0 2881.0 jit_solution(6452315681025738710)
XLA Ops:
  11.9 43.5 %all-reduce.11 = (bf16[6144]{0:T(1024)(128)(2,1)S(1)}, bf16[2048]{0:T(1024)(128)(2,1)S(1)}, bf16[2048]{0:T(1024)(128)(2,1)S(1)}, bf16[2048]{0:T(1024)(128)(2,1)S(1)}, bf16[2048]{0:T(1024)(128)(2,1)S(1)}) all-reduce(bf16[6144]{0:T(1024)(128)(2,1)S(1)} %dynamic-update-slice.2, ...), channel_id=1, replica_groups=mesh['seq'=2,'shard'=16] {'seq','shard'}, use_global_device_ids=true, to_apply=%add.2 | all-reduce | flops 14336 | bytes 57344
  56.3 113.5 %all-gather.6.cloned.1.call-done = bf16[2048,6144]{1,0:T(8,128)(2,1)} async-done(((bf16[64,6144]{1,0:T(8,128)(2,1)}), bf16[2048,6144]{1,0:T(8,128)(2,1)}) %all-gather.6.cloned.1.call-update) | async-done | bytes 25165840 | tf_op jit(solution)/shard_map/all_gather | solution.py:122
  169.8 10.5 convolution_add_fusion
  180.3 1.9 fusion.77
  183.1 2.2 reshape.249
  185.3 3.3 reshape.251
  190.8 2.0 subtract_convert_fusion.2
  192.7 2.4 pad_maximum_fusion
  196.7 2.3 copy.90
  199.0 3.9 all-to-all-start
  204.6 9.4 all-to-all-done
  214.0 3.5 all-to-all-start.1
  219.8 12.1 all-to-all-done.1
  231.9 4.3 all-to-all-start.2
  238.5 1.7 copy.96
  240.2 2.4 copy.93
  244.0 2.4 copy.97
  246.4 2.9 all-to-all-done.2
  249.3 2.4 copy.95
  253.2 2.4 copy.98
  255.7 39.9 %while.26 = (s32[]{:T(128)}, bf16[16,320,64]{1,2,0:T(8,128)(2,1)S(1)}, f32[16,320]{1,0:T(8,128)S(1)}, bf16[16,320,64]{2,1,0:T(8,128)(2,1)S(1)}, bf16[16,320,64]{...) while((s32[]{:T(128)}, bf16[16,320,64]{1,2,0:T(8,128)(2,1)S(1)}, ...), condition=%wide.region_5.6_spmd, body=%wide.region_2.5_spmd.sunk | while | flops 27156160 | bytes 1624665 | solution.py:152
  296.2 1.9 reduce.3
  300.7 3.5 all-to-all-start.3
  304.3 17.0 all-to-all-done.3
  323.0 5.3 fusion.78
  329.0 84.4 %all-gather.10.cloned.1.call-done = bf16[2048,5632]{1,0:T(8,128)(2,1)} async-done(((bf16[64,5632]{1,0:T(8,128)(2,1)}), bf16[2048,5632]{1,0:T(8,128)(2,1)}) %all-gather.10.cloned.1.call-update) | async-done | bytes 23068688 | tf_op jit(solution)/shard_map/all_gather | solution.py:160
  413.4 11.4 fusion.79
  424.8 134.2 %all-gather.12.cloned.1.call-done = bf16[2048,5632]{1,0:T(8,128)(2,1)} async-done(((bf16[64,5632]{1,0:T(8,128)(2,1)}), bf16[2048,5632]{1,0:T(8,128)(2,1)}) %all-gather.12.cloned.1.call-update) | async-done | bytes 23068688 | tf_op jit(solution)/shard_map/all_gather | solution.py:161
  559.0 11.4 fusion.80
  570.4 134.1 %all-gather.14.cloned.1.call-done = bf16[5632,2048]{1,0:T(8,128)(2,1)} async-done(((bf16[176,2048]{1,0:T(8,128)(2,1)}), bf16[5632,2048]{1,0:T(8,128)(2,1)}) %all-gather.14.cloned.1.call-update) | async-done | bytes 23068688 | tf_op jit(solution)/shard_map/all_gather | solution.py:162
  704.5 15.6 multiply_convert_fusion.1
  720.2 12.5 fusion.81
  732.7 14.5 multiply_reduce_fusion.1
  747.2 2.2 multiply_add_fusion
  749.4 8.2 fusion.70
  757.6 6.3 convolution_convert_fusion.2
  764.0 12.5 all_to_all.108
  779.1 91.8 %while.27 = (s32[]{:T(128)}, bf16[16,320,64]{1,2,0:T(8,128)(2,1)S(1)}, bf16[16,320,64]{1,2,0:T(8,128)(2,1)S(1)}, bf16[16,320,64]{1,2,0:T(8,128)(2,1)S(1)}, bf16[...) while((s32[]{:T(128)}, ...), condition=%wide.region_12.13_spmd, body=%wide.region_10.12_spmd.sunk | while | flops 66662080 | bytes 3902825 | solution.py:229
  870.9 1.9 reduce.5
  875.5 4.3 all-to-all-start.6
  882.5 6.7 all-to-all-done.6
  889.1 4.3 all-to-all-start.5
  898.9 1.8 convert_element_type.153
  902.4 4.3 all-to-all-start.7
  906.7 2.4 reshape.277
  912.2 3.4 convert_element_type.148
  915.6 1.7 convert_element_type.149
  917.3 3.0 subtract_convert_fusion
  923.2 1.8 convert_element_type.155
  925.1 2.9 pad_maximum_fusion.2
  928.0 1.8 convert_element_type.150
  934.5 19.9 fusion.73
  955.9 18.0 fusion.82
  975.5 26.9 fusion.83
  1002.4 1.8 copy-done.14
  1004.6 27.9 fusion.66
  1034.1 16.2 fusion.49
  1050.7 16.1 fusion.64
  1066.8 63.0 %all-reduce.10 = (f32[2048]{0:T(1024)S(1)}, f32[2048]{0:T(1024)S(1)}, f32[6144]{0:T(1024)S(1)}, f32[2048]{0:T(1024)S(1)}, f32[2048]{0:T(1024)S(1)}) all-reduce(f32[2048]{0:T(1024)S(1)} %get-tuple-element.161, f32[2048]{0:T(1024)S(1)} %get-tuple-element.166, ...), channel_id=2, replica_groups=mesh['seq'=2,'shard'=16] {'seq','shard'}, use_global_device_ids=true, to_apply=%region_16.17.clone | all-reduce | flops 14336 | bytes 114688
  1132.8 2.9 fusion.63
  1135.8 272.3 %reduce-scatter.6.cloned.1.call-done = f32[64,6144]{1,0:T(8,128)} async-done(((f32[2048,6144]{1,0:T(8,128)}), f32[64,6144]{1,0:T(8,128)}) %reduce-scatter.6.cloned.1.call-update) | async-done | bytes 1572880 | tf_op jit(solution)/shard_map/reduce_scatter | solution.py:266
  1408.1 483.5 %reduce-scatter.10.cloned.1.call-done = f32[64,5632]{1,0:T(8,128)} async-done(((f32[2048,5632]{1,0:T(8,128)}), f32[64,5632]{1,0:T(8,128)}) %reduce-scatter.10.cloned.1.call-update) | async-done | bytes 1441808 | tf_op jit(solution)/shard_map/reduce_scatter | solution.py:208
  1891.5 491.3 %reduce-scatter.12.cloned.1.call-done = f32[64,5632]{1,0:T(8,128)} async-done(((f32[2048,5632]{1,0:T(8,128)}), f32[64,5632]{1,0:T(8,128)}) %reduce-scatter.12.cloned.1.call-update) | async-done | bytes 1441808 | tf_op jit(solution)/shard_map/reduce_scatter | solution.py:209
  2382.9 491.2 %reduce-scatter.14.cloned.1.call-done = f32[176,2048]{1,0:T(8,128)} async-done(((f32[5632,2048]{1,0:T(8,128)}), f32[176,2048]{1,0:T(8,128)}) %reduce-scatter.14.cloned.1.call-update) | async-done | bytes 1441808 | tf_op jit(solution)/shard_map/reduce_scatter | solution.py:183
  (380 shorter events, 189.1 us)
Async XLA Ops:
  7.2 162.6 %all-gather.6.cloned.1.call-start = ((), (), s32[]{:S(2)}) async-start(), calls=%async_computation.13 | async-start | bytes 25952256 | tf_op jit(solution)/shard_map/all_gather | solution.py:122
  7.9 2.7 copy-start.25
  7.9 3.0 copy-start.26
  7.9 3.2 copy-start.27
  7.9 3.5 copy-start.28
  8.0 3.7 copy-start.29
  8.0 315.0 %all-gather.8.cloned.1.call-start = ((), (), s32[]{:S(2)}) async-start(), calls=%async_computation.14 | async-start | bytes 8650752 | tf_op jit(solution)/shard_map/all_gather | solution.py:124
  8.7 47.1 %copy-start.5 = (bf16[1,160,2048]{2,1,0:T(8,128)(2,1)S(1)}, bf16[1,160,2048]{2,1,0:T(8,128)(2,1)}, u32[]{:S(2)}) copy-start(bf16[1,160,2048]{2,1,0:T(8,128)(2,1)} %param.16) | copy-start | bytes 1966084
  8.7 404.7 %all-gather.10.cloned.1.call-start = ((), (), s32[]{:S(2)}) async-start(), calls=%async_computation.15 | async-start | bytes 23789568 | tf_op jit(solution)/shard_map/all_gather | solution.py:160
  9.5 549.5 %all-gather.12.cloned.1.call-start = ((), (), s32[]{:S(2)}) async-start(), calls=%async_computation.16 | async-start | bytes 23789568 | tf_op jit(solution)/shard_map/all_gather | solution.py:161
  10.0 694.5 %all-gather.14.cloned.1.call-start = ((), (), s32[]{:S(2)}) async-start(), calls=%async_computation.17 | async-start | bytes 23789568 | tf_op jit(solution)/shard_map/all_gather | solution.py:162
  180.3 2.8 copy-start.15
  188.6 1.8 copy-start
  199.0 15.0 all-to-all-start
  214.0 17.9 all-to-all-start.1
  231.9 4.3 copy-start.18
  231.9 17.5 all-to-all-start.2
  295.6 3.9 copy-start.13
  300.7 20.6 all-to-all-start.3
  304.2 831.5 %reduce-scatter.8.cloned.1.call-start = ((), (), s32[]{:S(2)}) async-start(), calls=%async_computation.19 | async-start | bytes 17301504 | tf_op jit(solution)/shard_map/reduce_scatter | solution.py:222
  323.0 5.4 copy-start.11
  328.4 418.9 %copy-start.3 = (f32[160,2048]{1,0:T(8,128)}, f32[160,2048]{1,0:T(8,128)S(1)}, u32[]{:S(2)}) copy-start(f32[160,2048]{1,0:T(8,128)S(1)} %get-tuple-element.232) | copy-start | bytes 3932164
  424.8 279.7 %copy-start.16 = (bf16[1,160,2048]{2,1,0:T(8,128)(2,1)S(1)}, bf16[1,160,2048]{2,1,0:T(8,128)(2,1)}, u32[]{:S(2)}) copy-start(bf16[1,160,2048]{2,1,0:T(8,128)(2,1)} %param.17) | copy-start | bytes 1966084
  747.2 2.2 copy-start.12
  749.4 8.2 copy-start.1
  875.5 13.6 all-to-all-start.6
  889.1 13.2 all-to-all-start.5
  902.4 27.4 all-to-all-start.7
  906.7 501.4 %reduce-scatter.6.cloned.1.call-start = ((), (), s32[]{:S(2)}) async-start(), calls=%async_computation.18 | async-start | bytes 51904512 | tf_op jit(solution)/shard_map/reduce_scatter | solution.py:266
  917.3 3.0 copy-start.7
  920.3 1.3 copy-start.8
  931.6 1.1 copy-start.20
  932.3 1.1 copy-start.19
  933.4 1.1 copy-start.6
  934.5 19.9 copy-start.9
  954.4 1.5 copy-start.22
  954.5 937.1 %reduce-scatter.10.cloned.1.call-start = ((), (), s32[]{:S(2)}) async-start(), calls=%async_computation.20 | async-start | bytes 47579136 | tf_op jit(solution)/shard_map/reduce_scatter | solution.py:208
  974.0 1.5 copy-start.21
  974.0 1408.9 %reduce-scatter.12.cloned.1.call-start = ((), (), s32[]{:S(2)}) async-start(), calls=%async_computation.21 | async-start | bytes 47579136 | tf_op jit(solution)/shard_map/reduce_scatter | solution.py:209
  1002.4 1.9 copy-start.14
  1002.4 2.2 copy-start.17
  1002.4 1871.6 %reduce-scatter.14.cloned.1.call-start = ((), (), s32[]{:S(2)}) async-start(), calls=%async_computation.22 | async-start | bytes 47579136 | tf_op jit(solution)/shard_map/reduce_scatter | solution.py:183
  1032.5 1.6 copy-start.4
  1034.1 16.2 copy-start.10
  1050.7 16.1 copy-start.23
  1050.7 16.1 copy-start.24
  1050.7 82.1 %copy-start.2 = (f32[160,2048]{1,0:T(8,128)S(1)}, f32[160,2048]{1,0:T(8,128)}, u32[]{:S(2)}) copy-start(f32[160,2048]{1,0:T(8,128)} %copy-done.1) | copy-start | bytes 3932164
Sparse Core Ops, SparseCore 0:
  10.9 158.8 all-gather.5
  172.7 87.7 all-gather.7
  263.4 150.0 all-gather.9
  416.2 142.7 all-gather.11
  561.7 142.7 all-gather.13
  757.7 181.9 reduce-scatter.7
  954.6 453.4 reduce-scatter.5
  1411.0 480.5 reduce-scatter.9
  1894.4 488.3 reduce-scatter.11
  2385.6 488.3 reduce-scatter.13
where the time goes:
time: 2900 us; the launch traced here: 2880 us
  waiting for transfers between devices  2260 us (78%)
  matrix products  347 us (12%)
  blocking collectives  119 us (4%)
  local copies, waits for them, and re-layouts  83.8 us (3%)
  other arithmetic  30.4 us (1%)
    reduce_scatter x1, waiting for transfers between devices, per_device(): lax.psum_scatter(grad_up_weight, ('seq', 'shard'), scatter_dimension=0, t...  491 us
    reduce_scatter x1, waiting for transfers between devices, per_device(): lax.psum_scatter(grad_down_weight, ('seq', 'shard'), scatter_dimension=0,...  491 us
    reduce_scatter x1, waiting for transfers between devices, per_device(): lax.psum_scatter(grad_gate_weight, ('seq', 'shard'), scatter_dimension=0,...  483 us
    reduce_scatter x1, waiting for transfers between devices, per_device(): lax.psum_scatter(grad_qkv_weight, ('seq', 'shard'), scatter_dimension=0,...  272 us
    all_gather x1, waiting for transfers between devices, per_device(): lax.all_gather(up_weight, ('seq', 'shard'), axis=0, tiled=True)  134 us
    all_gather x1, waiting for transfers between devices, per_device(): lax.all_gather(down_weight, ('seq', 'shard'), axis=0, tiled=True)  134 us
    all_gather x1, waiting for transfers between devices, per_device(): lax.all_gather(qkv_weight, ('seq', 'shard'), axis=0, tiled=True)  113 us
    unnamed x2, blocking collectives  107 us
  transfers between devices with their start and end apart: 17, of which 13 were waited for; matrix products, arithmetic and copies ran while one was open for 14% of the time, Pallas kernels for 0%

commit v1 on v0

v1 whole, which is shorter than its diff:
```python
import jax
import jax.numpy as jnp
import numpy as np
from jax import lax
from jax.sharding import PartitionSpec as P

HEADS = 32
HEAD_DIM = 64
ROTARY = 16
TEAM = ("seq", "zl")
PEERS = ("zh", "y", "c")
ALL = ("seq", "zh", "zl", "y", "c")
BF = jnp.bfloat16
F32 = jnp.float32


def norm_rows(values):
    centre = jnp.mean(values, axis=-1, keepdims=True)
    centred = values - centre
    spread = jnp.mean(centred * centred, axis=-1, keepdims=True)
    scale_rows = lax.rsqrt(spread + 1e-05)
    return (centred * scale_rows, scale_rows)


def norm_back(grad_normed, normed, scale_rows):
    return scale_rows * (
        grad_normed
        - jnp.mean(grad_normed, axis=-1, keepdims=True)
        - normed * jnp.mean(grad_normed * normed, axis=-1, keepdims=True)
    )


def rotate(values, positions, direction):
    halves = ROTARY // 2
    frequency = 10000.0 ** (-2.0 * jnp.arange(halves, dtype=F32) / ROTARY)
    angles = positions.astype(F32)[:, None] * frequency[None, :]
    cosine_table = jnp.cos(angles)[:, None, :]
    sine_table = jnp.sin(angles)[:, None, :] * direction
    first_half = values[..., :halves]
    second_half = values[..., halves:ROTARY]
    return jnp.concatenate(
        [
            first_half * cosine_table - second_half * sine_table,
            second_half * cosine_table + first_half * sine_table,
            values[..., ROTARY:],
        ],
        axis=-1,
    )


def dot(left, right):
    return jnp.dot(left, right, preferred_element_type=F32)


def dot_nt(left, right):
    return lax.dot_general(left, right, (((1,), (1,)), ((), ())), preferred_element_type=F32)


def dot_tn(left, right):
    return lax.dot_general(left, right, (((0,), (0,)), ((), ())), preferred_element_type=F32)


def per_device(
    tokens, cotangent, norm1_gain, norm1_bias, qkv_weight, qkv_bias, out_weight,
    norm2_gain, norm2_bias, gate_weight, up_weight, down_weight,
):
    zh = lax.axis_size("zh")
    rows = tokens.shape[1]
    width = tokens.shape[2]
    own = qkv_weight.shape[0]
    ff = gate_weight.shape[1]
    half = lax.axis_size("seq")
    length = rows * half
    team = half * lax.axis_size("zl")
    seqs = lax.axis_size("zl")

    def cut_columns(shard, parts):
        block = shard.shape[1] // parts // (half * zh * seqs)
        cut = shard.reshape(own, parts, half, zh, seqs, block).transpose(2, 4, 0, 1, 3, 5)
        return cut.reshape(team, own, parts * zh * block)

    def join_columns(cut, parts):
        block = cut.shape[2] // parts // zh
        cut = cut.reshape(half, seqs, own, parts, zh, block).transpose(2, 3, 0, 4, 1, 5)
        return cut.reshape(own, -1)

    def mine_columns(whole, parts):
        block = whole.shape[0] // parts // (half * zh * seqs)
        cut = whole.reshape(parts, half, zh, seqs, block)
        cut = lax.dynamic_index_in_dim(cut, lax.axis_index("seq"), 1, keepdims=False)
        cut = lax.dynamic_index_in_dim(cut, lax.axis_index("zl"), 2, keepdims=False)
        return cut.reshape(-1)

    def to_owner_order(values):
        n = values.shape[0]
        return values.reshape(n, half, zh, seqs, 4, own).transpose(0, 2, 4, 1, 3, 5).reshape(n, width)

    def from_owner_order(values):
        n = values.shape[0]
        return values.reshape(n, zh, 4, half, seqs, own).transpose(0, 3, 1, 4, 2, 5).reshape(n, width)

    def gather_columns(shard, parts):
        cut = cut_columns(shard, parts)
        cut = lax.all_to_all(cut, TEAM, split_axis=0, concat_axis=0, tiled=True)
        return lax.all_gather(cut.reshape(team * own, -1), PEERS, axis=0, tiled=True)

    def gather_rows(shard):
        return lax.all_gather(shard, PEERS, axis=0, tiled=True)

    def gather_tokens(values):
        return lax.all_gather(values, ("zl", "seq"), axis=0, tiled=True)

    def sum_tokens(values):
        return lax.psum_scatter(values.astype(BF), ("zl", "seq"), scatter_dimension=0, tiled=True).astype(F32)

    def sum_rows(values):
        return lax.psum_scatter(values.astype(BF), PEERS, scatter_dimension=0, tiled=True)

    def sum_columns(values, parts):
        part = sum_rows(values).reshape(team, own, -1)
        part = lax.all_to_all(part, TEAM, split_axis=0, concat_axis=0, tiled=True)
        return join_columns(part, parts).astype(F32)

    small = jnp.concatenate([norm1_gain, norm1_bias, norm2_gain, norm2_bias, qkv_bias])
    small = lax.all_gather(small, ALL, axis=0, tiled=False)
    first_gain = small[:, :own].reshape(-1).astype(F32)
    first_bias = small[:, own : 2 * own].reshape(-1).astype(F32)
    second_gain = small[:, 2 * own : 3 * own].reshape(-1).astype(F32)
    second_bias = small[:, 3 * own : 4 * own].reshape(-1).astype(F32)
    qkv_offset = mine_columns(small[:, 4 * own :].reshape(-1), 3).astype(F32)

    inputs = tokens[0].astype(F32)
    first_normed, first_scale = norm_rows(inputs)
    first_own = to_owner_order((first_normed * first_gain + first_bias).astype(BF))
    first_input = gather_tokens(first_own)
    qkv_matrix = gather_columns(qkv_weight, 3)
    out_matrix = gather_rows(out_weight)
    gate_matrix = gather_columns(gate_weight, 1)
    up_matrix = gather_columns(up_weight, 1)
    down_matrix = gather_rows(down_weight)
    upstream = gather_tokens(cotangent[0])

    projected = dot(first_input, qkv_matrix) + qkv_offset
    part = width // team
    group_heads = part // HEAD_DIM
    positions = jnp.tile(jnp.arange(length, dtype=jnp.int32), seqs)

    def heads_of(values):
        return values.reshape(seqs, length, group_heads, HEAD_DIM).transpose(0, 2, 1, 3)

    def unheads(values):
        return values.transpose(0, 2, 1, 3).reshape(seqs * length, part)

    queries = heads_of(rotate(projected[:, :part].reshape(-1, group_heads, HEAD_DIM), positions, 1.0).astype(BF))
    keys = heads_of(rotate(projected[:, part : 2 * part].reshape(-1, group_heads, HEAD_DIM), positions, 1.0).astype(BF))
    values = heads_of(projected[:, 2 * part :].astype(BF))
    causal = jnp.arange(length)[:, None] >= jnp.arange(length)[None, :]
    scores = jnp.einsum("shqd,shkd->shqk", queries, keys, preferred_element_type=F32) * 0.125
    scores = jnp.where(causal, scores, -1e30)
    highest = jnp.max(scores, axis=-1, keepdims=True)
    exponent = jnp.exp(scores - highest)
    probs = exponent / jnp.sum(exponent, axis=-1, keepdims=True)
    probs_low = probs.astype(BF)
    mixed = unheads(jnp.einsum("shqk,shkd->shqd", probs_low, values, preferred_element_type=F32).astype(BF))
    middle = inputs + sum_tokens(dot(mixed, out_matrix))

    second_normed, second_scale = norm_rows(middle)
    second_own = to_owner_order((second_normed * second_gain + second_bias).astype(BF))
    second_input = gather_tokens(second_own)
    gate_rows = dot(second_input, gate_matrix)
    up_rows = dot(second_input, up_matrix)
    sigmoid_gate = jax.nn.sigmoid(gate_rows)
    silu_gate = gate_rows * sigmoid_gate
    hidden = (silu_gate * up_rows).astype(BF)
    result = middle + sum_tokens(dot(hidden, down_matrix))

    down_total = sum_rows(dot_tn(hidden, upstream)).astype(F32)
    grad_hidden = dot_nt(upstream, down_matrix)
    grad_gate = (grad_hidden * up_rows * sigmoid_gate * (1.0 + gate_rows * (1.0 - sigmoid_gate))).astype(BF)
    grad_up = (grad_hidden * silu_gate).astype(BF)
    gate_total = sum_columns(dot_tn(second_input, grad_gate), 1)
    up_total = sum_columns(dot_tn(second_input, grad_up), 1)
    grad_second = from_owner_order(sum_tokens(dot_nt(grad_gate, gate_matrix) + dot_nt(grad_up, up_matrix)))
    grad_middle = cotangent[0].astype(F32) + norm_back(grad_second * second_gain, second_normed, second_scale)
    grad_attended = gather_tokens(grad_middle.astype(BF))
    out_total = sum_rows(dot_tn(mixed, grad_attended)).astype(F32)
    grad_mixed = heads_of(dot_nt(grad_attended, out_matrix).astype(BF))
    grad_probs = jnp.einsum("shqd,shkd->shqk", grad_mixed, values, preferred_element_type=F32)
    grad_scores = (probs * (grad_probs - jnp.sum(probs * grad_probs, axis=-1, keepdims=True))).astype(BF)
    grad_queries = (jnp.einsum("shqk,shkd->shqd", grad_scores, keys, preferred_element_type=F32) * 0.125).astype(BF)
    grad_keys = (jnp.einsum("shqk,shqd->shkd", grad_scores, queries, preferred_element_type=F32) * 0.125).astype(BF)
    grad_values = jnp.einsum("shqk,shqd->shkd", probs_low, grad_mixed, preferred_element_type=F32).astype(BF)
    grad_queries = rotate(unheads(grad_queries).astype(F32).reshape(-1, group_heads, HEAD_DIM), positions, -1.0)
    grad_keys = rotate(unheads(grad_keys).astype(F32).reshape(-1, group_heads, HEAD_DIM), positions, -1.0)
    grad_projected = jnp.concatenate(
        [grad_queries.reshape(-1, part).astype(BF), grad_keys.reshape(-1, part).astype(BF), unheads(grad_values)],
        axis=1,
    )
    qkv_total = sum_columns(dot_tn(first_input, grad_projected), 3)
    grad_first = from_owner_order(sum_tokens(dot_nt(grad_projected, qkv_matrix)))
    grad_inputs = grad_middle + norm_back(grad_first * first_gain, first_normed, first_scale)

    bias_part = jnp.sum(grad_projected.astype(F32), axis=0).reshape(3, zh, -1)
    bias_whole = jnp.zeros((3, half, zh, seqs, bias_part.shape[2]), F32)
    bias_whole = lax.dynamic_update_slice(
        bias_whole, bias_part[:, None, :, None], (0, lax.axis_index("seq"), 0, lax.axis_index("zl"), 0)
    ).reshape(-1)
    count = width // own
    sums = jnp.concatenate(
        [
            jnp.sum(grad_first * first_normed, axis=0).reshape(count, own),
            jnp.sum(grad_first, axis=0).reshape(count, own),
            jnp.sum(grad_second * second_normed, axis=0).reshape(count, own),
            jnp.sum(grad_second, axis=0).reshape(count, own),
            bias_whole.reshape(count, 3 * own),
        ],
        axis=1,
    )
    sums = lax.psum_scatter(sums, ALL, scatter_dimension=0, tiled=True)[0]
    return (
        result.astype(BF)[None],
        grad_inputs[None],
        sums[:own],
        sums[own : 2 * own],
        qkv_total,
        sums[4 * own :],
        out_total,
        sums[2 * own : 3 * own],
        sums[3 * own : 4 * own],
        gate_total,
        up_total,
        down_total,
    )


def solution(mesh):
    half, shards = mesh.shape["seq"], mesh.shape["shard"]
    fine = jax.sharding.Mesh(mesh.devices.reshape(half, shards // 8, 2, 2, 2), ALL)
    token = P(("zh", "zl", "y", "c"), "seq", None)
    row = P(ALL)
    return jax.shard_map(
        per_device,
        mesh=fine,
        in_specs=(token, token) + (row,) * 10,
        out_specs=(token, token) + (row,) * 10,
        check_vma=False,
    )
```

time: 2900 us -> 1320 us (0.46)
  waiting for transfers between devices: 2260 us -> 851 us
  matrix products: 347 us -> 150 us
  blocking collectives: 119 us -> 157 us
    reduce_scatter x5 -> x9, waiting for transfers between devices: 1740 us -> 454 us  [the longest x5 287 us: sum_rows(): lax.psum_scatter(values.astype(BF), PEERS, scatter_dimension=0, tiled=True)]
    dot_general x127 -> x20, matrix products: 347 us -> 142 us  [the longest x5 41.1 us: dot_tn(): lax.dot_general(left, right, (((0,), (0,)), ((), ())), preferred_element_...]
    all_gather x5 -> x9, waiting for transfers between devices: 466 us -> 394 us  [the longest x3 171 us: gather_columns(): lax.all_gather(cut.reshape(team * own, -1), PEERS, axis=0, tiled=True)]
    all_to_all x1 -> x3, blocking collectives: 12.5 us -> 73.3 us  [gather_columns(): cut = lax.all_to_all(cut, TEAM, split_axis=0, concat_axis=0, tiled=True)]
    all_to_all x7 -> x3, waiting for transfers between devices: 48.1 us -> 0.01 us  [sum_columns(): part = lax.all_to_all(part, TEAM, split_axis=0, concat_axis=0, tiled=True)]
  transfers between devices with their start and end apart: 17 -> 21, of which waited for: 13 -> 18; matrix products, arithmetic and copies ran while one was open for 14% -> 17% of each run, Pallas kernels for 0% -> 0%
where the time goes in v1:
time: 1320 us; the launch traced here: 1310 us
  waiting for transfers between devices  851 us (64%)
  blocking collectives  157 us (12%)
  matrix products  150 us (11%)
  local copies, waits for them, and re-layouts  88.6 us (7%)
  other arithmetic  40.3 us (3%)
  between operations  15.5 us (1%)
    reduce_scatter x5, waiting for transfers between devices, sum_rows(): lax.psum_scatter(values.astype(BF), PEERS, scatter_dimension=0, tiled=True)  287 us
    all_gather x3, waiting for transfers between devices, gather_columns(): lax.all_gather(cut.reshape(team * own, -1), PEERS, axis=0, tiled=True)  171 us
    reduce_scatter x4, waiting for transfers between devices, sum_tokens(): lax.psum_scatter(values.astype(BF), ('zl', 'seq'), scatter_dimension=0, t...  167 us
    all_gather x4, waiting for transfers between devices, gather_tokens(): return lax.all_gather(values, ('zl', 'seq'), axis=0, tiled=True)  151 us
    unnamed x2, blocking collectives  83.6 us
    all_to_all x3, blocking collectives, gather_columns(): cut = lax.all_to_all(cut, TEAM, split_axis=0, concat_axis=0, tiled=True)  73.3 us
    all_gather x2, waiting for transfers between devices, gather_rows(): return lax.all_gather(shard, PEERS, axis=0, tiled=True)  71.3 us
    dot_general x5, matrix products, dot_tn(): lax.dot_general(left, right, (((0,), (0,)), ((), ())), preferred_element_...  41.1 us
  transfers between devices with their start and end apart: 21, of which 18 were waited for; matrix products, arithmetic and copies ran while one was open for 17% of the time, Pallas kernels for 0%

profile of v1, /device:TPU:0, one launch (start us, length us, event | category | flops | bytes accessed | tf_op | source)
XLA Modules:
  0.0 1314.3 jit_solution(6410690791317332891)
XLA Ops:
  10.4 42.3 %all-reduce = bf16[14336]{0:T(1024)(128)(2,1)S(1)} all-reduce(bf16[14336]{0:T(1024)(128)(2,1)S(1)} %dynamic-update-slice), channel_id=2, replica_groups=mesh['seq'=2,'zh'=2,'zl'=2,'y'=2,'c'=2] {'seq','zh','zl','y','c'}, use_global_device_ids=true, to_apply=%add | all-reduce | flops 14336 | bytes 57344
  60.2 26.2 %all_to_all.30 = bf16[4,64,1536]{2,1,0:T(8,128)(2,1)} all-to-all(bf16[4,64,1536]{2,1,0:T(8,128)(2,1)S(1)} %reshape.408), channel_id=1, replica_groups=mesh['seq'=2,'zh'=2,'zl'=2,'y'=2,'c'=2] {'seq','zl'}, dimensions={0} | all-to-all | bytes 1572864 | tf_op jit(solution)/shard_map/all_to_all | solution.py:104
  88.3 27.7 %all-gather.12.cloned.1.call-done = bf16[640,2048]{1,0:T(8,128)(2,1)} async-done(((bf16[160,2048]{1,0:T(8,128)(2,1)}), bf16[640,2048]{1,0:T(8,128)(2,1)}) %all-gather.12.cloned.1.call-update) | async-done | bytes 2621456 | tf_op jit(solution)/shard_map/all_gather | solution.py:111
  116.0 73.4 %all-gather.14.cloned.1.call-done = bf16[2048,1536]{1,0:T(8,128)(2,1)} async-done(((bf16[256,1536]{1,0:T(8,128)(2,1)}), bf16[2048,1536]{1,0:T(8,128)(2,1)}) %all-gather.14.cloned.1.call-update) | async-done | bytes 6291472 | tf_op jit(solution)/shard_map/all_gather | solution.py:105
  189.4 7.1 convolution_add_fusion
  212.4 7.2 fusion.43
  219.7 4.1 fusion.24
  225.1 2.4 all-gather.16.cloned.1.call-done
  227.5 4.7 convolution_convert_fusion.6
  235.4 25.4 %all_to_all.31 = bf16[4,64,1408]{2,1,0:T(8,128)(2,1)} all-to-all(bf16[4,64,1408]{2,1,0:T(8,128)(2,1)S(1)} %reshape.417), channel_id=1, replica_groups=mesh['seq'=2,'zh'=2,'zl'=2,'y'=2,'c'=2] {'seq','zl'}, dimensions={0} | all-to-all | bytes 1441792 | tf_op jit(solution)/shard_map/all_to_all | solution.py:104
  261.0 29.4 %reduce-scatter.10.cloned.1.call-done = bf16[160,2048]{1,0:T(8,128)(2,1)} async-done(((bf16[640,2048]{1,0:T(8,128)(2,1)}), bf16[160,2048]{1,0:T(8,128)(2,1)}) %reduce-scatter.10.cloned.1.call-update) | async-done | bytes 655376 | tf_op jit(solution)/shard_map/reduce_scatter | solution.py:114
  297.6 21.6 %all_to_all.32 = bf16[4,64,1408]{2,1,0:T(8,128)(2,1)} all-to-all(bf16[4,64,1408]{2,1,0:T(8,128)(2,1)S(1)} %reshape.420), channel_id=1, replica_groups=mesh['seq'=2,'zh'=2,'zl'=2,'y'=2,'c'=2] {'seq','zl'}, dimensions={0} | all-to-all | bytes 1441792 | tf_op jit(solution)/shard_map/all_to_all | solution.py:104
  321.0 38.5 %all-gather.20.cloned.1.call-done = bf16[2048,1408]{1,0:T(8,128)(2,1)} async-done(((bf16[256,1408]{1,0:T(8,128)(2,1)}), bf16[2048,1408]{1,0:T(8,128)(2,1)}) %all-gather.20.cloned.1.call-update) | async-done | bytes 5767184 | tf_op jit(solution)/shard_map/all_gather | solution.py:105
  359.5 53.9 %all-gather.18.cloned.1.call-done = bf16[640,2048]{1,0:T(8,128)(2,1)} async-done(((bf16[160,2048]{1,0:T(8,128)(2,1)}), bf16[640,2048]{1,0:T(8,128)(2,1)}) %all-gather.18.cloned.1.call-update) | async-done | bytes 2621456 | tf_op jit(solution)/shard_map/all_gather | solution.py:111
  413.3 9.4 fusion.44
  422.8 59.5 %all-gather.22.cloned.1.call-done = bf16[2048,1408]{1,0:T(8,128)(2,1)} async-done(((bf16[256,1408]{1,0:T(8,128)(2,1)}), bf16[2048,1408]{1,0:T(8,128)(2,1)}) %all-gather.22.cloned.1.call-update) | async-done | bytes 5767184 | tf_op jit(solution)/shard_map/all_gather | solution.py:105
  482.2 9.4 fusion.45
  491.7 44.0 %all-gather.28.cloned.1.call-done = bf16[1,640,2048]{2,1,0:T(8,128)(2,1)} async-done(((bf16[1,160,2048]{2,1,0:T(8,128)(2,1)}), bf16[1,640,2048]{2,1,0:T(8,128)(2,1)}) %all-gather.28.cloned.1.call-update) | async-done | bytes 2621456 | tf_op jit(solution)/shard_map/all_gather | solution.py:111
  535.7 68.9 %all-gather.24.cloned.1.call-done = bf16[1408,2048]{1,0:T(8,128)(2,1)} async-done(((bf16[176,2048]{1,0:T(8,128)(2,1)}), bf16[1408,2048]{1,0:T(8,128)(2,1)}) %all-gather.24.cloned.1.call-update) | async-done | bytes 5767184 | tf_op jit(solution)/shard_map/all_gather | solution.py:108
  604.6 10.9 multiply_convert_fusion.1
  615.6 8.3 fusion.46
  623.9 5.6 add_convert_fusion
  630.0 8.1 convolution_convert_fusion.5
  638.2 41.7 %reduce-scatter.14.cloned.1.call-done = bf16[160,2048]{1,0:T(8,128)(2,1)} async-done(((bf16[640,2048]{1,0:T(8,128)(2,1)}), bf16[160,2048]{1,0:T(8,128)(2,1)}) %reduce-scatter.14.cloned.1.call-update) | async-done | bytes 655376 | tf_op jit(solution)/shard_map/reduce_scatter | solution.py:114
  682.8 2.7 copy.176
  687.9 45.6 %reduce-scatter.12.cloned.1.call-done = bf16[160,2048]{1,0:T(8,128)(2,1)} async-done(((bf16[640,2048]{1,0:T(8,128)(2,1)}), bf16[160,2048]{1,0:T(8,128)(2,1)}) %reduce-scatter.12.cloned.1.call-update) | async-done | bytes 655376 | tf_op jit(solution)/shard_map/reduce_scatter | solution.py:114
  733.5 4.0 fusion.41
  737.6 8.7 convolution_convert_fusion.2
  746.3 8.7 convolution_convert_fusion.1
  755.3 9.4 convolution_convert_fusion
  764.8 25.7 %all-gather.26.cloned.1.call-done = bf16[640,2048]{1,0:T(8,128)(2,1)} async-done(((bf16[160,2048]{1,0:T(8,128)(2,1)}), bf16[640,2048]{1,0:T(8,128)(2,1)}) %all-gather.26.cloned.1.call-update) | async-done | bytes 2621456 | tf_op jit(solution)/shard_map/all_gather | solution.py:111
  790.5 4.8 convolution_convert_fusion.8
  798.2 5.5 convolution_convert_fusion.7
  803.7 9.0 multiply_reduce_fusion
  812.7 9.9 multiply_convert_fusion
  823.7 3.0 fusion.27
  828.3 2.3 convert_element_type.358
  832.2 3.5 fusion.28
  837.4 2.3 convert_element_type.363
  841.4 4.7 fusion.21
  847.8 3.3 reshape.425
  853.6 8.7 convolution_convert_fusion.4
  863.4 8.7 convolution_convert_fusion.3
  872.2 4.3 reduce-scatter.22.cloned.1.call-done
  876.5 3.5 all-to-all-start.4
  880.0 82.1 %reduce-scatter.24.cloned.1.call-done = bf16[256,1408]{1,0:T(8,128)(2,1)} async-done(((bf16[2048,1408]{1,0:T(8,128)(2,1)}), bf16[256,1408]{1,0:T(8,128)(2,1)}) %reduce-scatter.24.cloned.1.call-update) | async-done | bytes 720912 | tf_op jit(solution)/shard_map/reduce_scatter | solution.py:117
  962.1 4.2 all-to-all-start.5
  968.7 78.7 %reduce-scatter.26.cloned.1.call-done = bf16[176,2048]{1,0:T(8,128)(2,1)} async-done(((bf16[1408,2048]{1,0:T(8,128)(2,1)}), bf16[176,2048]{1,0:T(8,128)(2,1)}) %reduce-scatter.26.cloned.1.call-update) | async-done | bytes 720912 | tf_op jit(solution)/shard_map/reduce_scatter | solution.py:117
  1047.4 2.4 convert_element_type.390
  1052.3 2.4 copy.220
  1054.7 3.6 reshape.444
  1058.3 2.7 reshape.450
  1060.9 2.4 copy.219
  1063.3 3.4 reshape.445
  1066.7 33.6 %reduce-scatter.20.cloned.1.call-done = bf16[64,2048]{1,0:T(8,128)(2,1)} async-done(((bf16[512,2048]{1,0:T(8,128)(2,1)}), bf16[64,2048]{1,0:T(8,128)(2,1)}) %reduce-scatter.20.cloned.1.call-update) | async-done | bytes 262160 | tf_op jit(solution)/shard_map/reduce_scatter | solution.py:117
  1102.1 50.7 %reduce-scatter.16.cloned.1.call-done = bf16[160,2048]{1,0:T(8,128)(2,1)} async-done(((bf16[640,2048]{1,0:T(8,128)(2,1)}), bf16[160,2048]{1,0:T(8,128)(2,1)}) %reduce-scatter.16.cloned.1.call-update) | async-done | bytes 655376 | tf_op jit(solution)/shard_map/reduce_scatter | solution.py:114
  1152.7 2.6 copy.187
  1155.4 88.3 %reduce-scatter.18.cloned.1.call-done = bf16[256,1536]{1,0:T(8,128)(2,1)} async-done(((bf16[2048,1536]{1,0:T(8,128)(2,1)}), bf16[256,1536]{1,0:T(8,128)(2,1)}) %reduce-scatter.18.cloned.1.call-update) | async-done | bytes 786448 | tf_op jit(solution)/shard_map/reduce_scatter | solution.py:117
  1243.7 3.5 all-to-all-start.3
  1247.2 3.5 fusion.9
  1253.4 41.3 %all-reduce.1 = f32[32,448]{1,0:T(8,128)S(1)} all-reduce(f32[32,448]{1,0:T(8,128)S(1)} %concatenate.51), channel_id=8, replica_groups=mesh['seq'=2,'zh'=2,'zl'=2,'y'=2,'c'=2] {'seq','zh','zl','y','c'}, use_global_device_ids=true, to_apply=%region_20.21.clone | all-reduce | flops 14336 | bytes 114688
  1297.2 3.3 add_bitcast_fusion
  1301.5 2.4 copy.221
  1303.9 3.4 reshape.443
  (252 shorter events, 76.5 us)
Async XLA Ops:
  7.2 46.4 %copy-start = (bf16[1,160,2048]{2,1,0:T(8,128)(2,1)S(1)}, bf16[1,160,2048]{2,1,0:T(8,128)(2,1)}, u32[]{:S(2)}) copy-start(bf16[1,160,2048]{2,1,0:T(8,128)(2,1)} %param.12) | copy-start | bytes 1966084
  7.2 2.9 copy-start.45
  7.2 2.9 copy-start.46
  7.2 2.9 copy-start.49
  7.2 2.9 copy-start.47
  7.2 2.9 copy-start.48
  7.2 108.7 %all-gather.12.cloned.1.call-start = ((), (), s32[]{:S(2)}) async-start(), calls=%async_computation.15 | async-start | bytes 3276800 | tf_op jit(solution)/shard_map/all_gather | solution.py:111
  10.0 46.2 %copy-start.1 = (f32[1,160,2048]{1,2,0:T(8,128)}, f32[1,160,2048]{1,2,0:T(8,128)S(1)}, u32[]{:S(2)}) copy-start(f32[1,160,2048]{1,2,0:T(8,128)S(1)} %copy.153) | copy-start | bytes 3932164
  53.5 2.7 copy-start.27
  55.2 3.3 copy-start.17
  58.4 131.0 %all-gather.14.cloned.1.call-start = ((), (), s32[]{:S(2)}) async-start(), calls=%async_computation.16 | async-start | bytes 7077888 | tf_op jit(solution)/shard_map/all_gather | solution.py:105
  59.6 27.6 %slice-start.2 = ((bf16[32,448]{1,0:T(8,128)(2,1)}), bf16[32,192]{1,0:T(8,128)(2,1)S(1)}, s32[]{:S(2)}) async-start(bf16[32,448]{1,0:T(8,128)(2,1)} %copy-done.29), calls=%async_computation.35 | async-start | bytes 32768 | tf_op jit(solution)/shard_map/slice | solution.py:130
  86.4 141.1 %all-gather.16.cloned.1.call-start = ((), (), s32[]{:S(2)}) async-start(), calls=%async_computation.17 | async-start | bytes 2359296 | tf_op jit(solution)/shard_map/all_gather | solution.py:108
  87.1 203.2 %reduce-scatter.10.cloned.1.call-start = ((), (), s32[]{:S(2)}) async-start(), calls=%async_computation.18 | async-start | bytes 3276800 | tf_op jit(solution)/shard_map/reduce_scatter | solution.py:114
  88.3 114.4 %copy-start.30 = (f32[640,8]{0,1:T(8,128)}, f32[640,8]{0,1:T(8,128)S(1)}, u32[]{:S(2)}) copy-start(f32[640,8]{0,1:T(8,128)S(1)} %get-tuple-element.48) | copy-start | bytes 61444
  199.1 3.5 copy-start.8
  207.0 3.7 copy-start.16
  209.2 3.1 copy-start.24
  212.4 7.2 copy-start.18
  219.6 4.1 copy-start.41
  225.1 7.1 copy-start.23
  232.2 127.2 %all-gather.20.cloned.1.call-start = ((), (), s32[]{:S(2)}) async-start(), calls=%async_computation.20 | async-start | bytes 6488064 | tf_op jit(solution)/shard_map/all_gather | solution.py:105
  234.8 26.1 %copy-start.38 = (f32[32,64]{1,0:T(8,128)S(1)}, f32[32,64]{1,0:T(8,128)}, u32[]{:S(2)}) copy-start(f32[32,64]{1,0:T(8,128)} %get-tuple-element.43) | copy-start | bytes 24580
  260.8 152.5 %all-gather.18.cloned.1.call-start = ((), (), s32[]{:S(2)}) async-start(), calls=%async_computation.19 | async-start | bytes 3276800 | tf_op jit(solution)/shard_map/all_gather | solution.py:111
  290.4 2.9 copy-start.4
  295.4 186.8 %all-gather.22.cloned.1.call-start = ((), (), s32[]{:S(2)}) async-start(), calls=%async_computation.21 | async-start | bytes 6488064 | tf_op jit(solution)/shard_map/all_gather | solution.py:105
  319.2 216.5 %all-gather.28.cloned.1.call-start = ((), (), s32[]{:S(2)}) async-start(), calls=%async_computation.32 | async-start | bytes 3276800 | tf_op jit(solution)/shard_map/all_gather | solution.py:111
  320.0 284.6 %all-gather.24.cloned.1.call-start = ((), (), s32[]{:S(2)}) async-start(), calls=%async_computation.22 | async-start | bytes 6488064 | tf_op jit(solution)/shard_map/all_gather | solution.py:108
  320.7 359.2 %reduce-scatter.14.cloned.1.call-start = ((), (), s32[]{:S(2)}) async-start(), calls=%async_computation.24 | async-start | bytes 3276800 | tf_op jit(solution)/shard_map/reduce_scatter | solution.py:114
  615.5 8.3 copy-start.51
  615.5 8.3 copy-start.52
  615.6 14.4 %copy-start.53 = (bf16[640,1408]{1,0:T(8,128)(2,1)}, bf16[640,1408]{1,0:T(8,128)(2,1)S(1)}, u32[]{:S(2)}) copy-start(bf16[640,1408]{1,0:T(8,128)(2,1)S(1)} %get-tuple-element.22) | copy-start | bytes 5406724
  615.6 8.3 copy-start.50
  629.5 104.0 %reduce-scatter.12.cloned.1.call-start = ((), (), s32[]{:S(2)}) async-start(), calls=%async_computation.23 | async-start | bytes 3276800 | tf_op jit(solution)/shard_map/reduce_scatter | solution.py:114
  638.1 152.4 %all-gather.26.cloned.1.call-start = ((), (), s32[]{:S(2)}) async-start(), calls=%async_computation.25 | async-start | bytes 3276800 | tf_op jit(solution)/shard_map/all_gather | solution.py:111
  737.5 139.0 %reduce-scatter.22.cloned.1.call-start = ((), (), s32[]{:S(2)}) async-start(), calls=%async_computation.29 | async-start | bytes 6488064 | tf_op jit(solution)/shard_map/reduce_scatter | solution.py:117
  746.3 215.8 %reduce-scatter.24.cloned.1.call-start = ((), (), s32[]{:S(2)}) async-start(), calls=%async_computation.30 | async-start | bytes 6488064 | tf_op jit(solution)/shard_map/reduce_scatter | solution.py:117
  755.1 292.3 %reduce-scatter.26.cloned.1.call-start = ((), (), s32[]{:S(2)}) async-start(), calls=%async_computation.31 | async-start | bytes 6488064 | tf_op jit(solution)/shard_map/reduce_scatter | solution.py:117
  764.8 335.5 %reduce-scatter.20.cloned.1.call-start = ((), (), s32[]{:S(2)}) async-start(), calls=%async_computation.28 | async-start | bytes 2359296 | tf_op jit(solution)/shard_map/reduce_scatter | solution.py:117
  798.2 5.5 copy-start.19
  803.7 9.0 copy-start.42
  822.6 330.1 %reduce-scatter.16.cloned.1.call-start = ((), (), s32[]{:S(2)}) async-start(), calls=%async_computation.26 | async-start | bytes 3276800 | tf_op jit(solution)/shard_map/reduce_scatter | solution.py:114
  828.3 3.5 copy-start.32
  830.6 5.1 copy-start.6
  830.6 1.5 copy-start.25
  830.6 1.6 copy-start.33
  837.4 3.6 copy-start.43
  839.7 1.7 copy-start.20
  846.0 5.1 copy-start.31
  846.0 5.1 copy-start.36
  846.1 6.4 slice-start
  851.1 2.5 copy-start.9
  862.4 381.3 %reduce-scatter.18.cloned.1.call-start = ((), (), s32[]{:S(2)}) async-start(), calls=%async_computation.27 | async-start | bytes 7077888 | tf_op jit(solution)/shard_map/reduce_scatter | solution.py:117
  872.2 94.2 %copy-start.28 = (f32[32,64]{1,0:T(8,128)S(1)}, f32[32,64]{1,0:T(8,128)}, u32[]{:S(2)}) copy-start(f32[32,64]{1,0:T(8,128)} %copy-done.27) | copy-start | bytes 24580
  872.2 94.8 %copy-start.39 = (f32[2048]{0:T(1024)S(1)}, f32[2048]{0:T(1024)}, u32[]{:S(2)}) copy-start(f32[2048]{0:T(1024)} %get-tuple-element.14) | copy-start | bytes 24580
  876.5 85.6 %all-to-all-start.4 = ((bf16[4,64,1408]{2,1,0:T(8,128)(2,1)}), bf16[4,64,1408]{2,1,0:T(8,128)(2,1)S(1)}, u32[]{:S(2)}, u32[]{:S(2)}) async-start(bf16[4,64,1408]{2,1,0:T(8,128)(2,1)} %bitcast.243), calls=%async_computation.11 | async-start | bytes 1441792 | tf_op jit(solution)/shard_map/all_to_all | solution.py:121
  962.1 96.1 %all-to-all-start.5 = ((bf16[4,64,1408]{2,1,0:T(8,128)(2,1)}), bf16[4,64,1408]{2,1,0:T(8,128)(2,1)}, u32[]{:S(2)}, u32[]{:S(2)}) async-start(bf16[4,64,1408]{2,1,0:T(8,128)(2,1)} %bitcast.242), calls=%async_computation.13 | async-start | bytes 1441792 | tf_op jit(solution)/shard_map/all_to_all | solution.py:121
  968.1 81.7 %copy-start.11 = (bf16[640,512]{0,1:T(8,128)(2,1)S(1)}, bf16[640,512]{0,1:T(8,128)(2,1)}, u32[]{:S(2)}) copy-start(bf16[640,512]{0,1:T(8,128)(2,1)} %reshape.425) | copy-start | bytes 1966084
  968.1 81.7 %copy-start.13 = (bf16[640,8,64]{0,2,1:T(8,128)(2,1)S(1)}, bf16[640,8,64]{0,2,1:T(8,128)(2,1)}, u32[]{:S(2)}) copy-start(bf16[640,8,64]{0,2,1:T(8,128)(2,1)} %copy-done.12) | copy-start | bytes 1966084
  968.1 81.7 %copy-start.15 = (bf16[640,8,64]{0,2,1:T(8,128)(2,1)S(1)}, bf16[640,8,64]{0,2,1:T(8,128)(2,1)}, u32[]{:S(2)}) copy-start(bf16[640,8,64]{0,2,1:T(8,128)(2,1)} %copy-done.14) | copy-start | bytes 1966084
  1102.1 145.1 %copy-start.2 = (f32[1,160,2048]{1,2,0:T(8,128)S(1)}, f32[1,160,2048]{1,2,0:T(8,128)}, u32[]{:S(2)}) copy-start(f32[1,160,2048]{1,2,0:T(8,128)} %copy-done.1) | copy-start | bytes 3932164
  1243.7 56.8 %all-to-all-start.3 = ((bf16[4,64,1536]{2,1,0:T(8,128)(2,1)}), bf16[4,64,1536]{2,1,0:T(8,128)(2,1)S(1)}, u32[]{:S(2)}, u32[]{:S(2)}) async-start(bf16[4,64,1536]{2,1,0:T(8,128)(2,1)} %bitcast.239), calls=%async_computation.8 | async-start | bytes 1572864 | tf_op jit(solution)/shard_map/all_to_all | solution.py:121
  1247.2 3.5 copy-start.3
  1250.8 1.6 copy-start.37
  (14 other events, 14.8 us)
Sparse Core Ops, SparseCore 0:
  58.5 57.4 all-gather.11
  117.9 71.4 all-gather.13
  191.3 36.1 all-gather.15
  232.3 57.9 reduce-scatter.9
  292.1 67.3 all-gather.19
  361.5 51.8 all-gather.17
  415.2 66.9 all-gather.21
  483.8 51.8 all-gather.27
  537.6 66.9 all-gather.23
  629.6 50.2 reduce-scatter.13
  682.2 51.2 reduce-scatter.11
  737.7 52.8 all-gather.25
  794.0 82.5 reduce-scatter.21
  880.2 81.8 reduce-scatter.23
  965.4 81.8 reduce-scatter.25
  1050.9 49.3 reduce-scatter.19
  1102.4 50.2 reduce-scatter.15
  1156.0 87.6 reduce-scatter.17

commit v2 on v1

--- a/solution.py
+++ b/solution.py
@@ -1,7 +1,8 @@
 import jax
 import jax.numpy as jnp
-import numpy as np
 from jax import lax
+from jax.experimental import pallas as pl
+from jax.experimental.pallas import tpu as pltpu
 from jax.sharding import PartitionSpec as P
 
 HEADS = 32
@@ -60,7 +61,7 @@
     return lax.dot_general(left, right, (((0,), (0,)), ((), ())), preferred_element_type=F32)
 
 
-def per_device(
+def plain_device(
     tokens, cotangent, norm1_gain, norm1_bias, qkv_weight, qkv_bias, out_weight,
     norm2_gain, norm2_bias, gate_weight, up_weight, down_weight,
 ):
@@ -233,15 +234,653 @@
     )
 
 
+MESH = pl.DeviceIdType.MESH
+ROWS = 16
+
+
+class Place:
+    def __init__(self, zhs):
+        self.s, self.zh, self.zl, self.y, self.c = (lax.axis_index(axis) for axis in ALL)
+        self.zhs = zhs
+
+    def at(self, **changed):
+        return tuple(changed.get(name, getattr(self, name)) for name in ("s", "zh", "zl", "y", "c"))
+
+    def mates(self):
+        for flip_s, flip_z in ((0, 1), (1, 0), (1, 1)):
+            yield (1 - self.s if flip_s else self.s), (1 - self.zl if flip_z else self.zl)
+
+    def highs(self):
+        for step in range(1, self.zhs):
+            yield (self.zh + step) % self.zhs
+
+    def greet(self):
+        partners = [self.at(s=s, zl=zl) for s, zl in self.mates()]
+        partners += [self.at(zh=zh) for zh in self.highs()]
+        partners += [self.at(y=1 - self.y), self.at(c=1 - self.c)]
+        barrier = pltpu.get_barrier_semaphore()
+        for partner in partners:
+            pl.semaphore_signal(barrier, inc=1, device_id=partner, device_id_type=MESH)
+        pl.semaphore_wait(barrier, len(partners))
+
+
+class Lines:
+    def __init__(self, send, recv, local):
+        self.send, self.recv, self.local = send, recv, local
+        self.sent, self.copied = [], 0
+
+    def push(self, source, target, device):
+        at = len(self.sent)
+        copy = pltpu.make_async_remote_copy(
+            src_ref=source, dst_ref=target, send_sem=self.send.at[at], recv_sem=self.recv.at[at],
+            device_id=device, device_id_type=MESH,
+        )
+        copy.start()
+        self.sent.append(copy)
+        return copy.wait_recv
+
+    def copy(self, source, target):
+        copy = pltpu.make_async_copy(source, target, self.local.at[self.copied])
+        copy.start()
+        self.copied += 1
+        return copy.wait
+
+    def finish(self):
+        for copy in self.sent:
+            copy.wait_send()
+
+
+def wait_all(waits):
+    for wait in waits:
+        wait()
+
+
+def run(*works):
+    works = list(works)
+    while works:
+        works = [work for work in works if next(work, works) is not works]
+
+
+def gather_team(lines, me, source, whole):
+    waits = [lines.copy(source, whole.at[me.zl, me.s])]
+    for s, zl in me.mates():
+        waits.append(lines.push(source, whole.at[me.zl, me.s], me.at(s=s, zl=zl)))
+    return waits
+
+
+def gather_columns(lines, me, cut, whole, other):
+    s = 1 - me.s if other else me.s
+    mine = whole.at[me.s, me.zh, me.zl, me.y, me.c]
+    waits = []
+    for flip in (0, 1):
+        zl = 1 - me.zl if flip else me.zl
+        if other or flip:
+            waits.append(lines.push(cut.at[s * 2 + zl], mine, me.at(s=s, zl=zl)))
+        else:
+            waits.append(lines.copy(cut.at[s * 2 + zl], mine))
+    yield
+    wait_all(waits)
+    part = whole.at[s, me.zh, :, me.y, me.c]
+    waits = [lines.push(part, part, me.at(zh=zh)) for zh in me.highs()]
+    yield
+    wait_all(waits)
+    part = whole.at[s, :, :, me.y, me.c]
+    wait = lines.push(part, part, me.at(y=1 - me.y))
+    yield
+    wait()
+    part = whole.at[s, :, :, :, me.c]
+    wait = lines.push(part, part, me.at(c=1 - me.c))
+    yield
+    wait()
+
+
+def gather_rows(lines, me, source, whole, start, size):
+    rows = pl.ds(start, size)
+    mine = whole.at[me.zh, me.y, me.c, rows]
+    waits = [lines.copy(source.at[rows], mine)]
+    waits += [lines.push(source.at[rows], mine, me.at(zh=zh)) for zh in me.highs()]
+    yield
+    wait_all(waits)
+    part = whole.at[:, me.y, me.c, rows]
+    wait = lines.push(part, part, me.at(y=1 - me.y))
+    yield
+    wait()
+    part = whole.at[:, :, me.c, rows]
+    wait = lines.push(part, part, me.at(c=1 - me.c))
+    yield
+    wait()
+
+
+def add_into(target, sources, result=None):
+    result = target if result is None else result
+
+    def step(at, carry):
+        rows = pl.ds(pl.multiple_of(at * ROWS, ROWS), ROWS)
+        total = target[rows].astype(F32)
+        for source in sources:
+            total = total + source[rows].astype(F32)
+        result[rows] = total.astype(result.dtype)
+        return carry
+
+    lax.fori_loop(0, target.shape[0] // ROWS, step, 0)
+
+
+def sum_columns(lines, me, grad, cut, buffers, other):
+    mine, first, second, third = buffers
+    s = 1 - me.s if other else me.s
+    loaded = lines.copy(grad.at[s, :, :, :, me.c], mine)
+    wait = lines.push(grad.at[s, :, :, :, 1 - me.c], first, me.at(c=1 - me.c))
+    yield
+    loaded()
+    wait()
+    for y in (1 - me.y, me.y):
+        for zh in range(me.zhs):
+            for zl in range(2):
+                add_into(mine.at[zh, zl, y], [first.at[zh, zl, y]])
+        if y is not me.y:
+            wait = lines.push(mine.at[:, :, y], second, me.at(y=y))
+    yield
+    wait()
+    waits = []
+    for step, zh in enumerate([*me.highs(), me.zh]):
+        for zl in range(2):
+            add_into(mine.at[zh, zl, me.y], [second.at[zh, zl]])
+        if step < me.zhs - 1:
+            waits.append(lines.push(mine.at[zh, :, me.y], third.at[step], me.at(zh=zh)))
+    yield
+    wait_all(waits)
+    for zl in range(2):
+        add_into(mine.at[me.zh, zl, me.y], [third.at[step, zl] for step in range(me.zhs - 1)])
+    waits = []
+    for flip in (0, 1):
+        zl = 1 - me.zl if flip else me.zl
+        source, target = mine.at[me.zh, zl, me.y], cut.at[me.s * 2 + me.zl]
+        if other or flip:
+            waits.append(lines.push(source, target, me.at(s=s, zl=zl)))
+        else:
+            waits.append(lines.copy(source, target))
+    yield
+    wait_all(waits)
+
+
+def sum_rows(lines, me, grad, total, buffers, start):
+    mine, first, second, third, final = buffers
+    rows = pl.ds(start, final.shape[0])
+    loaded = lines.copy(grad.at[:, :, me.c, rows], mine)
+    wait = lines.push(grad.at[:, :, 1 - me.c, rows], first, me.at(c=1 - me.c))
+    yield
+    loaded()
+    wait()
+    for y in (1 - me.y, me.y):
+        for zh in range(me.zhs):
+            add_into(mine.at[zh, y], [first.at[zh, y]])
+        if y is not me.y:
+            wait = lines.push(mine.at[:, y], second, me.at(y=y))
+    yield
+    wait()
+    waits = []
+    for step, zh in enumerate([*me.highs(), me.zh]):
+        add_into(mine.at[zh, me.y], [second.at[zh]])
+        if step < me.zhs - 1:
+            waits.append(lines.push(mine.at[zh, me.y], third.at[step], me.at(zh=zh)))
+    yield
+    wait_all(waits)
+    add_into(mine.at[me.zh, me.y], [third.at[step] for step in range(me.zhs - 1)], final)
+    wait = lines.copy(final, total.at[rows])
+    yield
+    wait()
+
+
+def sum_team(lines, me, partial, own, taken):
+    waits = []
+    for step, (s, zl) in enumerate(me.mates()):
+        waits.append(lines.push(partial.at[zl, s], taken.at[step], me.at(s=s, zl=zl)))
+    waits.append(lines.copy(partial.at[me.zl, me.s], own))
+    return waits
+
+
+def team_total(own, taken, rows):
+    total = own[rows].astype(F32)
+    for step in range(3):
+        total = total + taken[step, rows].astype(F32)
+    return total
+
+
+def by_rows(count, body):
+    def step(at, carry):
+        body(pl.ds(pl.multiple_of(at * ROWS, ROWS), ROWS))
+        return carry
+
+    lax.fori_loop(0, count // ROWS, step, 0)
+
+
+def halves(size):
+    first = (size // ROWS + 1) // 2 * ROWS
+    return ((0, first), (first, size - first)) if size > first else ((0, size),)
+
+
+def enter_kernel(zhs, tokens, small, qkv_cut, out, tokens_all, small_all, qkv_all, out_all, send, recv, local):
+    me, lines = Place(zhs), Lines(send, recv, local)
+    me.greet()
+    waits = gather_team(lines, me, tokens, tokens_all)
+    run(
+        gather_rows(lines, me, out, out_all, 0, out.shape[0]),
+        gather_columns(lines, me, qkv_cut, qkv_all, False),
+        gather_columns(lines, me, qkv_cut, qkv_all, True),
+        gather_columns(lines, me, small, small_all, False),
+        gather_columns(lines, me, small, small_all, True),
+    )
+    wait_all(waits)
+    lines.finish()
+
+
+def middle_kernel(
+    zhs, tokens, partial, upstream, gate_cut, up_cut, down, gain, bias,
+    middle, input_all, upstream_all, gate_all, up_all, down_all,
+    own, taken, second, send, recv, local,
+):
+    me, lines = Place(zhs), Lines(send, recv, local)
+    me.greet()
+    waits = sum_team(lines, me, partial, own, taken)
+    late = []
+
+    def tokens_work():
+        yield
+        wait_all(waits)
+
+        def body(rows):
+            values = tokens[rows].astype(F32) + team_total(own, taken, rows)
+            middle[rows] = values
+            second[rows] = (norm_rows(values)[0] * gain[...] + bias[...]).astype(BF)
+
+        by_rows(middle.shape[0], body)
+        late.extend(gather_team(lines, me, second, input_all))
+        late.extend(gather_team(lines, me, upstream, upstream_all))
+
+    run(
+        *[gather_rows(lines, me, down, down_all, start, size) for start, size in halves(down.shape[0])],
+        gather_columns(lines, me, gate_cut, gate_all, False),
+        gather_columns(lines, me, up_cut, up_all, False),
+        tokens_work(),
+        gather_columns(lines, me, gate_cut, gate_all, True),
+        gather_columns(lines, me, up_cut, up_all, True),
+    )
+    wait_all(late)
+    lines.finish()
+
+
+def back_kernel(
+    zhs, middle, upstream, gain, partial_down, partial_second, grad_down, grad_gate, grad_up,
+    result, grad_middle, sums, attended_all, down_total, gate_cut, up_cut,
+    own_down, taken_down, own_second, taken_second, attended, buffers, send, recv, local,
+):
+    me, lines = Place(zhs), Lines(send, recv, local)
+    me.greet()
+    waits = sum_team(lines, me, partial_second, own_second, taken_second)
+    late = []
+
+    def tokens_work():
+        yield
+        wait_all(waits)
+        late.extend(sum_team(lines, me, partial_down, own_down, taken_down))
+        sums[...] = jnp.zeros_like(sums)
+
+        def body(rows):
+            normed, scale_rows = norm_rows(middle[rows])
+            grad = team_total(own_second, taken_second, rows)
+            sums[0:1] += jnp.sum(grad * normed, axis=0, keepdims=True)
+            sums[1:2] += jnp.sum(grad, axis=0, keepdims=True)
+            grad = upstream[rows].astype(F32) + norm_back(grad * gain[...], normed, scale_rows)
+            grad_middle[rows] = grad
+            attended[rows] = grad.astype(BF)
+
+        by_rows(middle.shape[0], body)
+        shared = gather_team(lines, me, attended, attended_all)
+        yield
+        wait_all(late)
+
+        def last(rows):
+            result[rows] = (middle[rows] + team_total(own_down, taken_down, rows)).astype(BF)
+
+        by_rows(middle.shape[0], last)
+        yield
+        wait_all(shared)
+
+    pieces = halves(down_total.shape[0])
+    run(
+        *[
+            sum_rows(lines, me, grad_down, down_total, buffers[at], start)
+            for at, (start, size) in enumerate(pieces)
+        ],
+        tokens_work(),
+        sum_columns(lines, me, grad_gate, gate_cut, buffers[len(pieces)], False),
+        sum_columns(lines, me, grad_up, up_cut, buffers[len(pieces) + 1], False),
+        sum_columns(lines, me, grad_gate, gate_cut, buffers[len(pieces) + 2], True),
+        sum_columns(lines, me, grad_up, up_cut, buffers[len(pieces) + 3], True),
+    )
+    lines.finish()
+
+
+def leave_kernel(
+    zhs, tokens, grad_middle, gain, partial, vector, grad_out, grad_qkv,
+    grad_inputs, sums, out_total, qkv_cut,
+    own, taken, steps, buffers, send, recv, local,
+):
+    me, lines = Place(zhs), Lines(send, recv, local)
+    me.greet()
+    waits = sum_team(lines, me, partial, own, taken)
+
+    def tokens_work():
+        yield
+        wait_all(waits)
+        steps[0] = vector[...]
+
+        def body(rows):
+            normed, scale_rows = norm_rows(tokens[rows].astype(F32))
+            grad = team_total(own, taken, rows)
+            steps[0, 0:1] += jnp.sum(grad * normed, axis=0, keepdims=True)
+            steps[0, 1:2] += jnp.sum(grad, axis=0, keepdims=True)
+            grad_inputs[rows] = grad_middle[rows] + norm_back(grad * gain[...], normed, scale_rows)
+
+        by_rows(tokens.shape[0], body)
+        groups = [
+            [me.at(s=1 - me.s)], [me.at(zl=1 - me.zl)], [me.at(c=1 - me.c)], [me.at(y=1 - me.y)],
+            [me.at(zh=zh) for zh in me.highs()],
+        ]
+        at = 0
+        for group in groups:
+            arrived = [
+                lines.push(steps.at[at], steps.at[at + 1 + number], device)
+                for number, device in enumerate(group)
+            ]
+            yield
+            wait_all(arrived)
+            total = steps[at]
+            for number in range(len(group)):
+                total = total + steps[at + 1 + number]
+            at += len(group) + 1
+            steps[at] = total
+        sums[...] = steps[at]
+
+    pieces = halves(out_total.shape[0])
+    run(
+        *[
+            sum_rows(lines, me, grad_out, out_total, buffers[at], start)
+            for at, (start, size) in enumerate(pieces)
+        ],
+        tokens_work(),
+        sum_columns(lines, me, grad_qkv, qkv_cut, buffers[len(pieces)], False),
+        sum_columns(lines, me, grad_qkv, qkv_cut, buffers[len(pieces) + 1], True),
+    )
+    lines.finish()
+
+
+def row_buffers(zhs, size, width):
+    return tuple(
+        pltpu.VMEM(shape + (size, width), BF) for shape in ((zhs, 2), (zhs, 2), (zhs,), (zhs - 1,))
+    ) + (pltpu.VMEM((size, width), F32),)
+
+
+def column_buffers(zhs, own, columns):
+    return tuple(
+        pltpu.VMEM(shape + (own, columns), BF)
+        for shape in ((zhs, 2, 2), (zhs, 2, 2), (zhs, 2), (zhs - 1, 2))
+    )
+
+
+IN_HBM = pl.BlockSpec(memory_space=pl.ANY)
+IN_VMEM = pl.BlockSpec(memory_space=pltpu.VMEM)
+
+
+def call(kernel, zhs, number, inputs, outputs, scratch, copies, locals_, limit):
+    return pl.pallas_call(
+        lambda *refs: kernel(zhs, *refs),
+        out_shape=[jax.ShapeDtypeStruct(shape, kind) for shape, kind, _ in outputs],
+        in_specs=[spec for _, spec in inputs],
+        out_specs=[spec for _, _, spec in outputs],
+        scratch_shapes=[
+            *scratch,
+            pltpu.SemaphoreType.DMA((copies,)),
+            pltpu.SemaphoreType.DMA((copies,)),
+            pltpu.SemaphoreType.DMA((locals_,)),
+        ],
+        compiler_params=pltpu.CompilerParams(
+            collective_id=number, has_side_effects=True, vmem_limit_bytes=limit << 20
+        ),
+    )(*[array for array, _ in inputs])
+
+
+def per_device(
+    tokens, cotangent, norm1_gain, norm1_bias, qkv_weight, qkv_bias, out_weight,
+    norm2_gain, norm2_bias, gate_weight, up_weight, down_weight,
+):
+    zh = lax.axis_size("zh")
+    rows = tokens.shape[1]
+    width = tokens.shape[2]
+    own = qkv_weight.shape[0]
+    ff = gate_weight.shape[1]
+    ff_own = down_weight.shape[0]
+    half = lax.axis_size("seq")
+    length = rows * half
+    seqs = lax.axis_size("zl")
+    team = half * seqs
+    part = width // team
+    ff_part = ff // team
+    devices = width // own
+    tokens, cotangent = tokens[0], cotangent[0]
+    index = (lax.axis_index("seq") * (devices // half)
+             + ((lax.axis_index("zh") * 2 + lax.axis_index("zl")) * 2 + lax.axis_index("y")) * 2
+             + lax.axis_index("c"))
+
+    def cut_columns(shard, parts):
+        block = shard.shape[1] // parts // (half * zh * seqs)
+        cut = shard.reshape(own, parts, half, zh, seqs, block).transpose(2, 4, 0, 1, 3, 5)
+        return cut.reshape(team, own, parts * zh * block)
+
+    def join_columns(cut, parts):
+        block = cut.shape[2] // parts // zh
+        cut = cut.reshape(half, seqs, own, parts, zh, block).transpose(2, 3, 0, 4, 1, 5)
+        return cut.reshape(own, -1).astype(F32)
+
+    def mine_columns(whole, parts):
+        block = whole.shape[0] // parts // (half * zh * seqs)
+        cut = whole.reshape(parts, half, zh, seqs, block)
+        cut = lax.dynamic_index_in_dim(cut, lax.axis_index("seq"), 1, keepdims=False)
+        cut = lax.dynamic_index_in_dim(cut, lax.axis_index("zl"), 2, keepdims=False)
+        return cut.reshape(-1)
+
+    small = jnp.concatenate([norm1_gain, norm1_bias, norm2_gain, norm2_bias, qkv_bias]).astype(F32)
+    small = jnp.pad(small, (0, 1024 - small.shape[0])).reshape(8, 128)
+    small = jnp.broadcast_to(small, (team, 8, 128))
+    token_shape = (seqs, half, rows, width)
+    owners = (half, zh, seqs, 2, 2)
+    tokens_all, small_all, qkv_all, out_all = call(
+        enter_kernel, zh, 0,
+        [(tokens, IN_HBM), (small, IN_HBM), (cut_columns(qkv_weight, 3), IN_HBM), (out_weight, IN_HBM)],
+        [
+            (token_shape, BF, IN_HBM),
+            (owners + (8, 128), F32, IN_HBM),
+            (owners + (own, 3 * part), BF, IN_HBM),
+            ((zh, 2, 2, own, width), BF, IN_HBM),
+        ],
+        [], 12 + 5 * (zh + 4), 8, 16,
+    )
+    small = small_all.reshape(devices, 1024)
+    first_gain = small[:, :own].reshape(1, width)
+    first_bias = small[:, own : 2 * own].reshape(1, width)
+    second_gain = small[:, 2 * own : 3 * own].reshape(1, width)
+    second_bias = small[:, 3 * own : 4 * own].reshape(1, width)
+    qkv_offset = mine_columns(small[:, 4 * own : 7 * own].reshape(-1), 3)
+    qkv_matrix = qkv_all.reshape(width, 3 * part)
+    out_matrix = out_all.reshape(part, width)
+
+    first_input = (
+        norm_rows(tokens_all.reshape(-1, width).astype(F32))[0] * first_gain + first_bias
+    ).astype(BF)
+    projected = dot(first_input, qkv_matrix) + qkv_offset
+    group_heads = part // HEAD_DIM
+    positions = jnp.tile(jnp.arange(length, dtype=jnp.int32), seqs)
+
+    def heads_of(values):
+        return values.reshape(seqs, length, group_heads, HEAD_DIM).transpose(0, 2, 1, 3)
+
+    def unheads(values):
+        return values.transpose(0, 2, 1, 3).reshape(seqs * length, part)
+
+    queries = heads_of(rotate(projected[:, :part].reshape(-1, group_heads, HEAD_DIM), positions, 1.0).astype(BF))
+    keys = heads_of(rotate(projected[:, part : 2 * part].reshape(-1, group_heads, HEAD_DIM), positions, 1.0).astype(BF))
+    values = heads_of(projected[:, 2 * part :].astype(BF))
+    causal = jnp.arange(length)[:, None] >= jnp.arange(length)[None, :]
+    scores = jnp.einsum("shqd,shkd->shqk", queries, keys, preferred_element_type=F32) * 0.125
+    scores = jnp.where(causal, scores, -1e30)
+    highest = jnp.max(scores, axis=-1, keepdims=True)
+    exponent = jnp.exp(scores - highest)
+    probs = exponent / jnp.sum(exponent, axis=-1, keepdims=True)
+    probs_low = probs.astype(BF)
+    mixed = unheads(jnp.einsum("shqk,shkd->shqd", probs_low, values, preferred_element_type=F32).astype(BF))
+    partial = dot(mixed, out_matrix).astype(BF).reshape(token_shape)
+
+    limit = 48
+    token_scratch = [pltpu.VMEM((rows, width), BF), pltpu.VMEM((3, rows, width), BF)]
+    middle, input_all, upstream_all, gate_all, up_all, down_all = call(
+        middle_kernel, zh, 1,
+        [
+            (tokens, IN_VMEM), (partial, IN_HBM), (cotangent, IN_HBM),
+            (cut_columns(gate_weight, 1), IN_HBM), (cut_columns(up_weight, 1), IN_HBM),
+            (down_weight, IN_HBM), (second_gain, IN_VMEM), (second_bias, IN_VMEM),
+        ],
+        [
+            ((rows, width), F32, IN_VMEM),
+            (token_shape, BF, IN_HBM),
+            (token_shape, BF, IN_HBM),
+            (owners + (own, ff_part), BF, IN_HBM),
+            (owners + (own, ff_part), BF, IN_HBM),
+            ((zh, 2, 2, ff_own, width), BF, IN_HBM),
+        ],
+        [*token_scratch, pltpu.VMEM((rows, width), BF)],
+        9 + 6 * (zh + 4), 16, limit,
+    )
+    second_input = input_all.reshape(-1, width)
+    upstream = upstream_all.reshape(-1, width)
+    gate_matrix = gate_all.reshape(width, ff_part)
+    up_matrix = up_all.reshape(width, ff_part)
+    down_matrix = down_all.reshape(ff_part, width)
+    gate_rows = dot(second_input, gate_matrix)
+    up_rows = dot(second_input, up_matrix)
+    sigmoid_gate = jax.nn.sigmoid(gate_rows)
+    silu_gate = gate_rows * sigmoid_gate
+    hidden = (silu_gate * up_rows).astype(BF)
+    partial_down = dot(hidden, down_matrix).astype(BF).reshape(token_shape)
+
+    grad_down = dot_tn(hidden, upstream).astype(BF).reshape(down_all.shape)
+    grad_hidden = dot_nt(upstream, down_matrix)
+    grad_gate = (grad_hidden * up_rows * sigmoid_gate * (1.0 + gate_rows * (1.0 - sigmoid_gate))).astype(BF)
+    grad_up = (grad_hidden * silu_gate).astype(BF)
+    partial_second = (dot_nt(grad_gate, gate_matrix) + dot_nt(grad_up, up_matrix)).astype(BF).reshape(token_shape)
+    pieces = [size for _, size in halves(ff_own)]
+    result, grad_middle, second_sums, attended_all, down_total, gate_cut, up_cut = call(
+        back_kernel, zh, 2,
+        [
+            (middle, IN_VMEM), (cotangent, IN_VMEM), (second_gain, IN_VMEM),
+            (partial_down, IN_HBM), (partial_second, IN_HBM), (grad_down, IN_HBM),
+            (dot_tn(second_input, grad_gate).astype(BF).reshape(gate_all.shape), IN_HBM),
+            (dot_tn(second_input, grad_up).astype(BF).reshape(up_all.shape), IN_HBM),
+        ],
+        [
+            ((rows, width), BF, IN_VMEM),
+            ((rows, width), F32, IN_VMEM),
+            ((8, width), F32, IN_VMEM),
+            (token_shape, BF, IN_HBM),
+            ((ff_own, width), F32, IN_HBM),
+            ((team, own, ff_part), BF, IN_HBM),
+            ((team, own, ff_part), BF, IN_HBM),
+        ],
+        [
+            *token_scratch, *token_scratch, pltpu.VMEM((rows, width), BF),
+            [row_buffers(zh, size, width) for size in pieces]
+            + [column_buffers(zh, own, ff_part) for _ in range(4)],
+        ],
+        9 + 6 * (zh + 4), 20, limit,
+    )
+
+    grad_attended = attended_all.reshape(-1, width)
+    grad_out = dot_tn(mixed, grad_attended).astype(BF).reshape(out_all.shape)
+    grad_mixed = heads_of(dot_nt(grad_attended, out_matrix).astype(BF))
+    grad_probs = jnp.einsum("shqd,shkd->shqk", grad_mixed, values, preferred_element_type=F32)
+    grad_scores = (probs * (grad_probs - jnp.sum(probs * grad_probs, axis=-1, keepdims=True))).astype(BF)
+    grad_queries = (jnp.einsum("shqk,shkd->shqd", grad_scores, keys, preferred_element_type=F32) * 0.125).astype(BF)
+    grad_keys = (jnp.einsum("shqk,shqd->shkd", grad_scores, queries, preferred_element_type=F32) * 0.125).astype(BF)
+    grad_values = jnp.einsum("shqk,shqd->shkd", probs_low, grad_mixed, preferred_element_type=F32).astype(BF)
+    grad_queries = rotate(unheads(grad_queries).astype(F32).reshape(-1, group_heads, HEAD_DIM), positions, -1.0)
+    grad_keys = rotate(unheads(grad_keys).astype(F32).reshape(-1, group_heads, HEAD_DIM), positions, -1.0)
+    grad_projected = jnp.concatenate(
+        [grad_queries.reshape(-1, part).astype(BF), grad_keys.reshape(-1, part).astype(BF), unheads(grad_values)],
+        axis=1,
+    )
+    partial_first = dot_nt(grad_projected, qkv_matrix).astype(BF).reshape(token_shape)
+    bias_part = jnp.sum(grad_projected.astype(F32), axis=0).reshape(3, zh, -1)
+    bias_whole = jnp.zeros((3, half, zh, seqs, bias_part.shape[2]), F32)
+    bias_whole = lax.dynamic_update_slice(
+        bias_whole, bias_part[:, None, :, None], (0, lax.axis_index("seq"), 0, lax.axis_index("zl"), 0)
+    ).reshape(3, width)
+    vector = jnp.concatenate(
+        [jnp.zeros((2, width), F32), second_sums[:2], bias_whole, jnp.zeros((1, width), F32)], axis=0
+    )
+    pieces = [size for _, size in halves(own)]
+    grad_inputs, sums, out_total, qkv_cut = call(
+        leave_kernel, zh, 3,
+        [
+            (tokens, IN_VMEM), (grad_middle, IN_VMEM), (first_gain, IN_VMEM),
+            (partial_first, IN_HBM), (vector, IN_VMEM), (grad_out, IN_HBM),
+            (dot_tn(first_input, grad_projected).astype(BF).reshape(qkv_all.shape), IN_HBM),
+        ],
+        [
+            ((rows, width), F32, IN_VMEM),
+            ((8, width), F32, IN_VMEM),
+            ((own, width), F32, IN_HBM),
+            ((team, own, 3 * part), BF, IN_HBM),
+        ],
+        [
+            *token_scratch, pltpu.VMEM((zh + 9, 8, width), F32),
+            [row_buffers(zh, size, width) for size in pieces]
+            + [column_buffers(zh, own, 3 * part) for _ in range(2)],
+        ],
+        3 + zh + 3 + 4 * (zh + 4), 12, limit,
+    )
+
+    def mine(vector_row, size):
+        return lax.dynamic_slice_in_dim(vector_row, index * size, size, 0)
+
+    return (
+        result[None],
+        grad_inputs[None],
+        mine(sums[0], own),
+        mine(sums[1], own),
+        join_columns(qkv_cut, 3),
+        mine(sums[4:7].reshape(-1), 3 * own),
+        out_total,
+        mine(sums[2], own),
+        mine(sums[3], own),
+        join_columns(gate_cut, 1),
+        join_columns(up_cut, 1),
+        down_total,
+    )
+
+
 def solution(mesh):
     half, shards = mesh.shape["seq"], mesh.shape["shard"]
     fine = jax.sharding.Mesh(mesh.devices.reshape(half, shards // 8, 2, 2, 2), ALL)
     token = P(("zh", "zl", "y", "c"), "seq", None)
     row = P(ALL)
-    return jax.shard_map(
-        per_device,
-        mesh=fine,
-        in_specs=(token, token) + (row,) * 10,
-        out_specs=(token, token) + (row,) * 10,
-        check_vma=False,
-    )
+
+    def program(*arguments):
+        whole_tiles = arguments[-1].shape[0] // (half * shards) % ROWS == 0
+        return jax.shard_map(
+            per_device if whole_tiles else plain_device,
+            mesh=fine,
+            in_specs=(token, token) + (row,) * 10,
+            out_specs=(token, token) + (row,) * 10,
+            check_vma=False,
+        )(*arguments)
+
+    return program

time: 1320 us -> 802 us (0.61)
  waiting for transfers between devices: 851 us -> 0 us
  Pallas kernels: 0 us -> 545 us
  blocking collectives: 157 us -> 0 us
  other arithmetic: 40.3 us -> 15.3 us
  between operations: 15.5 us -> 1.8 us
    pallas_call x0 -> x4, Pallas kernels: none -> 545 us  [call(): pl.pallas_call(lambda *refs: kernel(zhs, *refs), out_shape=[jax.ShapeDtyp...]
    reduce_scatter x9 -> x0, waiting for transfers between devices: 454 us -> none  [the longest x5 287 us: sum_rows(): lax.psum_scatter(values.astype(BF), PEERS, scatter_dimension=0, tiled=True)]
    all_gather x9 -> x0, waiting for transfers between devices: 394 us -> none  [the longest x3 171 us: gather_columns(): lax.all_gather(cut.reshape(team * own, -1), PEERS, axis=0, tiled=True)]
    unnamed x2 -> x0, blocking collectives: 83.6 us -> none
    all_to_all x3 -> x0, blocking collectives: 73.3 us -> none  [gather_columns(): cut = lax.all_to_all(cut, TEAM, split_axis=0, concat_axis=0, tiled=True)]
    convert_element_type x16 -> x9, local copies, waits for them, and re-layouts: 25.3 us -> 30.1 us  [join_columns(): return cut.reshape(own, -1).astype(F32)]
  transfers between devices with their start and end apart: 21 -> 0, of which waited for: 18 -> 0; matrix products, arithmetic and copies ran while one was open for 17% -> 0% of each run, Pallas kernels for 0% -> 0%
where the time goes in v2:
time: 802 us; the launch traced here: 793 us
  Pallas kernels  545 us (68%)
  matrix products  137 us (17%)
  local copies, waits for them, and re-layouts  93.9 us (12%)
  other arithmetic  15.3 us (2%)
    pallas_call x4, Pallas kernels, call(): pl.pallas_call(lambda *refs: kernel(zhs, *refs), out_shape=[jax.ShapeDtyp...  545 us
    dot_general x5, matrix products, dot_nt(): lax.dot_general(left, right, (((1,), (1,)), ((), ())), preferred_element_...  39.1 us
    dot_general x5, matrix products, dot(): return jnp.dot(left, right, preferred_element_type=F32)  35.7 us
    dot_general x5, matrix products, dot_tn(): lax.dot_general(left, right, (((0,), (0,)), ((), ())), preferred_element_...  35.2 us
    convert_element_type x9, local copies, waits for them, and re-layouts, join_columns(): return cut.reshape(own, -1).astype(F32)  30.1 us

profile of v2, /device:TPU:0, one launch (start us, length us, event | category | flops | bytes accessed | tf_op | source)
XLA Modules:
  0.0 792.7 jit_solution(2019822926623894933)
XLA Ops:
  1.8 3.4 concatenate.39
  6.8 2.6 reshape.335
  10.0 1.4 reshape.336.refs_2_
  11.3 0.9 reshape.345
  12.9 1.4 reshape.346.refs_3_
  14.3 0.9 reshape.347
  15.8 1.4 reshape.348.refs_4_
  17.2 1.1 copy-done.1
  18.4 108.8 %shard_map.211 = (bf16[2,2,160,2048]{3,2,1,0:T(8,128)(2,1)S(1)}, f32[2,2,2,2,2,8,128]{6,5,4,3,2,1,0:T(8,128)S(1)}, bf16[2,2,2,2,2,64,1536]{6,5,4,3,2,1,0:T(8,128)(2,1)S(1)}, bf16[2,2,2,64,2048]{4,3,2,1,0:T(8,128)(2,1)S(1)}) custom-call(bf16[160,2048]{1,0:T(8,128)(2,1)S(1)} %bitcast.165, f32[4,8,128]{2,1,0:T(8,128)S(1)} %broadcast_in_dim.21.refs_1_, ...), custom_call_target="tpu_custom_call" | custom-call | tf_op jit(solution)/shard_map/pallas_call | solution.py:636
  127.1 1.3 copy-done.13
  128.5 2.6 copy-done.12
  133.2 2.5 fusion.5
  135.6 1.0 add_convert_fusion.1
  136.7 6.6 convolution_add_fusion
  143.3 0.9 slice.148
  144.4 1.5 copy.37
  145.9 1.3 slice.150
  147.6 0.9 copy.40
  148.6 1.8 reshape.379
  150.4 1.6 copy.46
  152.4 1.1 subtract_convert_fusion.3
  156.1 6.9 fusion.44
  163.0 4.1 fusion.23
  167.1 1.7 copy.48
  168.8 2.9 reshape.342
  171.8 4.3 convolution_convert_fusion.6
  176.1 152.3 %shard_map.212 = (f32[160,2048]{1,0:T(8,128)S(1)}, bf16[2,2,160,2048]{3,2,1,0:T(8,128)(2,1)}, bf16[2,2,160,2048]{3,2,1,0:T(8,128)(2,1)}, bf16[2,2,2,2,2,64,1408]...) custom-call(bf16[160,2048]{1,0:T(8,128)(2,1)S(1)} %bitcast.166, ...), custom_call_target="tpu_custom_call" | custom-call | tf_op jit(solution)/shard_map/pallas_call | solution.py:636
  328.4 9.7 %fusion.46 = f32[640,1408]{1,0:T(8,128)} fusion(bf16[640,2048]{1,0:T(8,128)(2,1)} %bitcast.215, bf16[2048,1408]{1,0:T(8,128)(2,1)} %bitcast.207), kind=kOutput, calls=%fused_computation.99 | convolution fusion | flops 3690987520 | bytes 11993088 | tf_op jit(solution)/shard_map/dot_general | solution.py:53
  338.1 6.1 fusion.45
  344.2 12.8 %multiply_convert_fusion.1 = (bf16[640,1408]{1,0:T(8,128)(2,1)}, bf16[640,1408]{1,0:T(8,128)(2,1)S(1)}, bf16[640,1408]{1,0:T(8,128)(2,1)}) fusion(f32[640,1408]{1,0:T(8,128)} %fusion.45, f32[640,1408]{1,0:T(8,128)} %fusion.46, bf16[640,2048]{1,0:T(8,128)(2,1)} %bitcast.221, bf16[1408,2048]{1,0:T(8,128)(2,1)} %bitcast.213), kind=kOutput, calls=%fused_computation.24 | convolution fusion | flops 3704504320 | bytes 21004288 | tf_op jit(solution)/shard_map/dot_general | solution.py:57
  357.0 9.1 %convolution_convert_fusion.5 = bf16[640,2048]{1,0:T(8,128)(2,1)} fusion(bf16[640,1408]{1,0:T(8,128)(2,1)} %get-tuple-element.56, bf16[1408,2048]{1,0:T(8,128)(2,1)} %bitcast.214), kind=kOutput, calls=%fused_computation.31 | convolution fusion | flops 3692298240 | bytes 10190848 | tf_op jit(solution)/shard_map/dot_general | solution.py:53
  366.1 6.0 fusion.47
  372.1 7.5 add_convert_fusion
  379.6 6.5 convolution_convert_fusion.3
  386.2 6.8 convolution_convert_fusion.1
  393.0 6.9 convolution_convert_fusion.2
  400.0 185.7 %shard_map.213 = (bf16[160,2048]{1,0:T(8,128)(2,1)S(1)}, f32[160,2048]{1,0:T(8,128)S(1)}, f32[8,2048]{1,0:T(8,128)S(1)}, bf16[2,2,160,2048]{3,2,1,0:T(8,128)(2,1...) custom-call(f32[160,2048]{1,0:T(8,128)S(1)} %get-tuple-element.37.refs_0_, ...), custom_call_target="tpu_custom_call" | custom-call | tf_op jit(solution)/shard_map/pallas_call | solution.py:636
  585.7 0.9 copy-done.7
  586.6 4.1 convolution_convert_fusion.8
  590.7 2.2 copy.51
  592.9 3.0 reshape.363
  595.9 4.8 fusion.20
  600.7 1.7 copy.59
  602.4 2.9 reshape.364
  605.3 5.0 convolution_convert_fusion.7
  610.4 2.6 reshape.377
  612.9 3.8 copy.61
  616.8 3.6 reshape.374
  620.3 2.6 reshape.378
  622.9 3.9 copy.62
  626.8 3.4 reshape.375
  630.2 8.0 %multiply_reduce_fusion = (f32[2,8,320]{2,1,0:T(8,128)S(1)}, f32[2,8,320,320]{2,3,1,0:T(8,128)}) fusion(f32[2,8,320,320]{2,3,1,0:T(8,128)} %get-tuple-element.83, f32[2,8,320]{2,1,0:T(8,128)S(1)} %get-tuple-element.82, bf16[2,320,8,64]{1,3,2,0:T(8,128)(2,1)S(1)} %copy-done.19, bf16[2,8,320,64]{2,0,3,1:T(2,128)(2,1)} %bitcast.204), kind=kOutput, calls=%fused_computation.2 | convolution fusion | flops 214625280 | bytes 14458880 | tf_op jit(solution)/shard_map/shqd,shkd->shqk/dot_general | solution.py:809
  638.2 7.1 multiply_convert_fusion
  645.3 2.3 fusion.27
  649.8 2.8 copy.56
  652.7 2.4 convert_element_type.262
  656.4 8.7 %convolution_convert_fusion.4 = bf16[640,2048]{1,0:T(8,128)(2,1)} fusion(bf16[2048,1536]{1,0:T(8,128)(2,1)} %bitcast.174, bf16[640,512]{0,1:T(8,128)(2,1)S(1)} %copy-done.16, bf16[640,512]{0,1:T(8,128)(2,1)S(1)} %bitcast.196, bf16[640,512]{0,1:T(8,128)(2,1)S(1)} %bitcast.193), kind=kOutput, calls=%fused_computation.30 | convolution fusion | flops 4033740800 | bytes 10878976 | tf_op jit(solution)/shard_map/dot_general | solution.py:57
  665.6 9.8 %convolution_convert_fusion = bf16[2048,1536]{1,0:T(8,128)(2,1)} fusion(bf16[640,2048]{1,0:T(8,128)(2,1)} %fusion.5, bf16[640,512]{0,1:T(8,128)(2,1)} %reshape.364, bf16[640,512]{0,1:T(8,128)(2,1)S(1)} %bitcast.198, bf16[640,512]{0,1:T(8,128)(2,1)S(1)} %bitcast.195), kind=kOutput, calls=%fused_computation.5 | convolution fusion | flops 4035575808 | bytes 10878976 | tf_op jit(solution)/shard_map/dot_general | solution.py:61
  675.4 98.1 %shard_map.214 = (f32[160,2048]{1,0:T(8,128)S(1)}, f32[8,2048]{1,0:T(8,128)S(1)}, f32[64,2048]{1,0:T(8,128)S(1)}, bf16[4,64,1536]{2,1,0:T(8,128)(2,1)S(1)}) custom-call(bf16[160,2048]{1,0:T(8,128)(2,1)S(1)} %bitcast.167, f32[160,2048]{1,0:T(8,128)S(1)} %get-tuple-element.44.refs_1_, f32[1,2048]{1,0:T(1,128)S(1)} %reshape.361.refs_2_, ...), custom_call_target="tpu_custom_call" | custom-call | tf_op jit(solution)/shard_map/pallas_call | solution.py:636
  778.3 3.0 reshape.376
  781.2 3.9 copy.60
  785.1 3.4 reshape.373
  789.3 1.1 copy.92
  791.2 1.1 copy.94
  (157 shorter events, 20.7 us)
Async XLA Ops:
  0.6 10.7 %copy-start.20 = (bf16[64,5632]{1,0:T(8,128)(2,1)S(1)}, bf16[64,5632]{1,0:T(8,128)(2,1)}, u32[]{:S(2)}) copy-start(bf16[64,5632]{1,0:T(8,128)(2,1)} %param.21) | copy-start | bytes 2162692
  12.2 2.1 copy-start.21
  14.3 2.9 copy-start
  14.3 2.9 copy-start.11
  17.2 1.1 copy-start.1
  127.1 1.3 copy-start.13
  128.5 2.6 copy-start.12
  150.3 2.0 copy-start.26
  150.3 2.0 copy-start.35
  153.5 2.5 copy-start.22
  153.5 2.5 copy-start.27
  153.7 9.3 %copy-start.28 = (bf16[2,320,8,8]{1,3,2,0:T(8,128)(2,1)}, bf16[2,320,8,8]{1,3,2,0:T(8,128)(2,1)S(1)}, u32[]{:S(2)}) copy-start(bf16[2,320,8,8]{1,3,2,0:T(8,128)(2,1)S(1)} %copy.38) | copy-start | bytes 245764
  153.9 9.2 %copy-start.30 = (bf16[2,320,8,8]{1,3,2,0:T(8,128)(2,1)}, bf16[2,320,8,8]{1,3,2,0:T(8,128)(2,1)S(1)}, u32[]{:S(2)}) copy-start(bf16[2,320,8,8]{1,3,2,0:T(8,128)(2,1)S(1)} %copy.39) | copy-start | bytes 245764
  156.1 7.0 copy-start.24
  156.1 7.0 copy-start.18
  167.1 4.6 copy-start.14
  171.8 4.3 copy-start.2
  171.8 4.3 copy-start.3
  171.8 4.3 copy-start.4
  171.8 4.3 copy-start.6
  328.4 9.7 %copy-start.38 = (bf16[2,2,2,2,2,64,1408]{6,5,4,3,2,1,0:T(8,128)(2,1)S(1)}, bf16[2,2,2,2,2,64,1408]{6,5,4,3,2,1,0:T(8,128)(2,1)}, u32[]{:S(2)}) copy-start(bf16[2,2,2,2,2,64,1408]{6,5,4,3,2,1,0:T(8,128)(2,1)} %get-tuple-element.39) | copy-start | bytes 17301508
  328.4 9.7 %copy-start.39 = (bf16[2,2,160,2048]{3,2,1,0:T(8,128)(2,1)S(1)}, bf16[2,2,160,2048]{3,2,1,0:T(8,128)(2,1)}, u32[]{:S(2)}) copy-start(bf16[2,2,160,2048]{3,2,1,0:T(8,128)(2,1)} %get-tuple-element.38) | copy-start | bytes 7864324
  338.1 34.0 %slice-start = ((s8[5767168]{0:T(1024)(128)(4,1)}), s8[4194304]{0:T(1024)(128)(4,1)S(1)}, s32[]{:S(2)}) async-start(s8[5767168]{0:T(1024)(128)(4,1)} %bitcast.208), calls=%async_computation | async-start | bytes 8388608
  344.2 27.9 %slice-start.1 = ((s8[5767168]{0:T(1024)(128)(4,1)}), s8[1572864]{0:T(1024)(128)(4,1)S(1)}, s32[]{:S(2)}) async-start(s8[5767168]{0:T(1024)(128)(4,1)} %bitcast.208), calls=%async_computation.1 | async-start | bytes 3145728
  366.1 6.0 copy-start.41
  372.1 7.5 copy-start.40
  372.1 7.5 copy-start.42
  400.0 186.6 %copy-start.15 = (bf16[2,2,2,64,2048]{4,3,2,1,0:T(8,128)(2,1)S(1)}, bf16[2,2,2,64,2048]{4,3,2,1,0:T(8,128)(2,1)}, u32[]{:S(2)}) copy-start(bf16[2,2,2,64,2048]{4,3,2,1,0:T(8,128)(2,1)} %copy-done.13) | copy-start | bytes 6291460
  585.7 0.9 copy-start.7
  622.9 7.3 copy-start.19
  638.2 7.1 copy-start.23
  638.2 7.1 copy-start.29
  638.2 7.1 copy-start.31
  645.3 2.3 copy-start.25
  645.3 2.3 copy-start.32
  645.3 2.3 copy-start.33
  655.2 0.7 copy-start.34
  655.3 1.1 copy-start.16
  656.4 9.1 %copy-start.36 = (f32[8]{0:T(128)S(1)}, f32[8]{0:T(128)}, u32[]{:S(2)}) copy-start(f32[8]{0:T(128)} %pad.9.clone) | copy-start | bytes 100
  656.4 9.1 %copy-start.37 = (f32[8]{0:T(128)S(1)}, f32[8]{0:T(128)}, u32[]{:S(2)}) copy-start(f32[8]{0:T(128)} %pad.6.clone) | copy-start | bytes 100
  773.5 0.9 copy-start.5
  774.4 0.8 copy-start.9
  781.2 7.2 copy-start.8
  788.5 1.9 copy-start.10
  788.5 2.7 copy-start.17

commit v3 on v2

--- a/solution.py
+++ b/solution.py
@@ -1,5 +1,6 @@
 import jax
 import jax.numpy as jnp
+import numpy as np
 from jax import lax
 from jax.experimental import pallas as pl
 from jax.experimental.pallas import tpu as pltpu
@@ -236,6 +237,7 @@
 
 MESH = pl.DeviceIdType.MESH
 ROWS = 16
+QKV_PARTS, OUT_PARTS, FF_PARTS, DOWN_PARTS = 2, 2, 2, 4
 
 
 class Place:
@@ -295,40 +297,58 @@
         wait()
 
 
-def run(*works):
-    works = list(works)
-    while works:
-        works = [work for work in works if next(work, works) is not works]
-
-
-def gather_team(lines, me, source, whole):
-    waits = [lines.copy(source, whole.at[me.zl, me.s])]
-    for s, zl in me.mates():
-        waits.append(lines.push(source, whole.at[me.zl, me.s], me.at(s=s, zl=zl)))
-    return waits
-
-
-def gather_columns(lines, me, cut, whole, other):
-    s = 1 - me.s if other else me.s
-    mine = whole.at[me.s, me.zh, me.zl, me.y, me.c]
+def run(*plan, spawned=()):
+    plan, opened, turn = list(plan), [], 0
+    while plan or opened or spawned:
+        opened = [*spawned, *[work for start, work in plan if start == turn], *opened]
+        if spawned:
+            spawned.clear()
+        plan = [item for item in plan if item[0] != turn]
+        opened = [work for work in opened if next(work, run) is not run]
+        turn += 1
+
+
+def rest(turns):
+    for _ in range(turns):
+        yield
+
+
+def gather_team(lines, me, source, whole, turns):
+    mine, other = whole.at[me.zl, me.s], whole.at[1 - me.zl, me.s]
+    waits = [
+        lines.copy(source, mine),
+        lines.push(source, mine, me.at(s=1 - me.s)),
+    ]
+    across = lines.push(source, mine, me.at(zl=1 - me.zl))
+    yield from rest(turns)
+    across()
+    waits.append(lines.push(other, other, me.at(s=1 - me.s)))
+    yield from rest(turns)
+    wait_all(waits)
+
+
+def gather_columns(lines, me, cut, whole, piece):
+    other, start, size = piece
+    s, columns = 1 - me.s if other else me.s, pl.ds(start, size)
+    mine = whole.at[me.s, me.zh, me.zl, me.y, me.c, :, columns]
     waits = []
     for flip in (0, 1):
         zl = 1 - me.zl if flip else me.zl
         if other or flip:
-            waits.append(lines.push(cut.at[s * 2 + zl], mine, me.at(s=s, zl=zl)))
+            waits.append(lines.push(cut.at[s * 2 + zl, :, columns], mine, me.at(s=s, zl=zl)))
         else:
-            waits.append(lines.copy(cut.at[s * 2 + zl], mine))
+            waits.append(lines.copy(cut.at[s * 2 + zl, :, columns], mine))
     yield
     wait_all(waits)
-    part = whole.at[s, me.zh, :, me.y, me.c]
+    part = whole.at[s, me.zh, :, me.y, me.c, :, columns]
     waits = [lines.push(part, part, me.at(zh=zh)) for zh in me.highs()]
     yield
     wait_all(waits)
-    part = whole.at[s, :, :, me.y, me.c]
+    part = whole.at[s, :, :, me.y, me.c, :, columns]
     wait = lines.push(part, part, me.at(y=1 - me.y))
     yield
     wait()
-    part = whole.at[s, :, :, :, me.c]
+    part = whole.at[s, :, :, :, me.c, :, columns]
     wait = lines.push(part, part, me.at(c=1 - me.c))
     yield
     wait()
@@ -365,11 +385,12 @@
     lax.fori_loop(0, target.shape[0] // ROWS, step, 0)
 
 
-def sum_columns(lines, me, grad, cut, buffers, other):
+def sum_columns(lines, me, grad, cut, buffers, piece):
     mine, first, second, third = buffers
-    s = 1 - me.s if other else me.s
-    loaded = lines.copy(grad.at[s, :, :, :, me.c], mine)
-    wait = lines.push(grad.at[s, :, :, :, 1 - me.c], first, me.at(c=1 - me.c))
+    other, start, size = piece
+    s, columns = 1 - me.s if other else me.s, pl.ds(start, size)
+    loaded = lines.copy(grad.at[s, :, :, :, me.c, :, columns], mine)
+    wait = lines.push(grad.at[s, :, :, :, 1 - me.c, :, columns], first, me.at(c=1 - me.c))
     yield
     loaded()
     wait()
@@ -394,7 +415,7 @@
     waits = []
     for flip in (0, 1):
         zl = 1 - me.zl if flip else me.zl
-        source, target = mine.at[me.zh, zl, me.y], cut.at[me.s * 2 + me.zl]
+        source, target = mine.at[me.zh, zl, me.y], cut.at[me.s * 2 + me.zl, :, columns]
         if other or flip:
             waits.append(lines.push(source, target, me.at(s=s, zl=zl)))
         else:
@@ -431,19 +452,25 @@
     wait()
 
 
-def sum_team(lines, me, partial, own, taken):
-    waits = []
-    for step, (s, zl) in enumerate(me.mates()):
-        waits.append(lines.push(partial.at[zl, s], taken.at[step], me.at(s=s, zl=zl)))
-    waits.append(lines.copy(partial.at[me.zl, me.s], own))
-    return waits
+def sum_team(lines, me, partial, own, passed, taken, turns):
+    first = [
+        lines.copy(partial.at[1 - me.zl, me.s], passed),
+        lines.push(partial.at[1 - me.zl, 1 - me.s], taken.at[0], me.at(s=1 - me.s)),
+    ]
+    waits = [
+        lines.push(partial.at[me.zl, 1 - me.s], taken.at[1], me.at(s=1 - me.s)),
+        lines.copy(partial.at[me.zl, me.s], own),
+    ]
+    yield from rest(turns)
+    wait_all(first)
+    add_into(passed, [taken.at[0]])
+    waits.append(lines.push(passed, taken.at[2], me.at(zl=1 - me.zl)))
+    yield from rest(turns)
+    wait_all(waits)
 
 
 def team_total(own, taken, rows):
-    total = own[rows].astype(F32)
-    for step in range(3):
-        total = total + taken[step, rows].astype(F32)
-    return total
+    return own[rows].astype(F32) + taken[1, rows].astype(F32) + taken[2, rows].astype(F32)
 
 
 def by_rows(count, body):
@@ -454,39 +481,174 @@
     lax.fori_loop(0, count // ROWS, step, 0)
 
 
-def halves(size):
-    first = (size // ROWS + 1) // 2 * ROWS
-    return ((0, first), (first, size - first)) if size > first else ((0, size),)
+def row_pieces(size, parts):
+    tiles, pieces, start = size // ROWS, [], 0
+    for part in range(parts):
+        count = (tiles * (part + 1) // parts - tiles * part // parts) * ROWS
+        pieces.append((start, count))
+        start += count
+    return pieces
+
+
+def column_pieces(columns, parts):
+    lanes, pieces, start = columns // 128, [], 0
+    for part in range(parts):
+        size = (lanes * (part + 1) // parts - lanes * part // parts) * 128
+        pieces.append((start, size))
+        start += size
+    return [(other, *piece) for other in (False, True) for piece in pieces]
+
+
+def turn_pairs(values, tables, sign):
+    return (
+        values * tables[0]
+        + pltpu.roll(values, 128 - ROTARY // 2, 1) * (tables[1] * sign)
+        + pltpu.roll(values, ROTARY // 2, 1) * (tables[2] * sign)
+    )
+
+
+def rotary_tables(length):
+    lane = np.arange(128) % HEAD_DIM
+    halves = ROTARY // 2
+    frequency = np.float32(10000.0) ** (np.float32(-2.0) * np.arange(halves, dtype=np.float32) / np.float32(ROTARY))
+    angles = np.arange(length, dtype=np.float32)[:, None] * frequency[lane % halves][None, :]
+    rotated = lane < ROTARY
+    return np.stack([
+        np.where(rotated, np.cos(angles), 1.0),
+        np.where(lane < halves, -np.sin(angles), 0.0),
+        np.where(rotated & (lane >= halves), np.sin(angles), 0.0),
+    ]).astype(np.float32)
+
+
+def lane_masks():
+    lane = lax.broadcasted_iota(jnp.int32, (1, 128), 1)
+    return [(lane < HEAD_DIM).astype(F32).astype(BF), (lane >= HEAD_DIM).astype(F32).astype(BF)], lane < HEAD_DIM
+
+
+def softmax_rows(query, key):
+    length = query.shape[0]
+    scores = dot_nt(query, key) * 0.125
+    below = lax.broadcasted_iota(jnp.int32, (length, length), 0) >= lax.broadcasted_iota(
+        jnp.int32, (length, length), 1
+    )
+    scores = jnp.where(below, scores, -1e30)
+    exponent = jnp.exp(scores - jnp.max(scores, axis=-1, keepdims=True))
+    return exponent / jnp.sum(exponent, axis=-1, keepdims=True)
+
+
+def pairs_of(seq, length, part, body):
+    def step(at, carry):
+        body(pl.ds(seq * length, length), pl.ds(pl.multiple_of(at * 128, 128), 128))
+        return carry
+
+    lax.fori_loop(0, part // 128, step, 0)
+
+
+def forward_attention(first, weight, offset, tables, queries, keys, values, mixed):
+    length, part = tables.shape[1], queries.shape[1]
+    seqs = queries.shape[0] // length
+    for number, target in enumerate((queries, keys, values)):
+        for start in range(0, part, 256):
+            at = number * part + start
+            block = dot(first[...], weight[:, at : at + 256]) + offset[:, at : at + 256]
+            if target is values:
+                target[:, start : start + 256] = block.astype(BF)
+                continue
+            for seq in range(seqs):
+                for lanes in range(0, 256, 128):
+                    rows = slice(seq * length, (seq + 1) * length)
+                    turned = turn_pairs(block[rows, lanes : lanes + 128], tables, 1.0)
+                    target[rows, start + lanes : start + lanes + 128] = turned.astype(BF)
+        yield
+
+    masks, left = lane_masks()
+    for seq in range(seqs):
+
+        def body(rows, lanes):
+            query, key, value = queries[rows, lanes], keys[rows, lanes], values[rows, lanes]
+            sides = [dot(softmax_rows(query * mask, key).astype(BF), value) for mask in masks]
+            mixed[rows, lanes] = jnp.where(left, *sides).astype(BF)
+
+        pairs_of(seq, length, part, body)
+        yield
+
+
+def backward_attention(grad_mixed, tables, queries, keys, values, grad_projected):
+    length, part = tables.shape[1], queries.shape[1]
+    seqs = queries.shape[0] // length
+    masks, left = lane_masks()
+    for seq in range(seqs):
+
+        def body(rows, lanes):
+            query, key, value = queries[rows, lanes], keys[rows, lanes], values[rows, lanes]
+            grad = grad_mixed[rows, lanes]
+            sides = []
+            for mask in masks:
+                probs = softmax_rows(query * mask, key)
+                grad_probs = dot_nt(grad * mask, value)
+                grad_scores = (
+                    probs * (grad_probs - jnp.sum(probs * grad_probs, axis=-1, keepdims=True))
+                ).astype(BF)
+                sides.append((
+                    dot(grad_scores, key) * 0.125,
+                    dot_tn(grad_scores, query) * 0.125,
+                    dot_tn(probs.astype(BF), grad),
+                ))
+            grads = [jnp.where(left, *pair).astype(BF) for pair in zip(*sides)]
+            start = lanes.start
+            for number, found in enumerate(grads):
+                if number < 2:
+                    found = turn_pairs(found.astype(F32), tables, -1.0).astype(BF)
+                grad_projected[rows, pl.ds(pl.multiple_of(start + number * part, 128), 128)] = found
+
+        pairs_of(seq, length, part, body)
+        yield
 
 
 def enter_kernel(zhs, tokens, small, qkv_cut, out, tokens_all, small_all, qkv_all, out_all, send, recv, local):
     me, lines = Place(zhs), Lines(send, recv, local)
     me.greet()
-    waits = gather_team(lines, me, tokens, tokens_all)
+    works = [gather_columns(lines, me, qkv_cut, qkv_all, piece) for piece in column_pieces(qkv_cut.shape[2], QKV_PARTS)]
     run(
-        gather_rows(lines, me, out, out_all, 0, out.shape[0]),
-        gather_columns(lines, me, qkv_cut, qkv_all, False),
-        gather_columns(lines, me, qkv_cut, qkv_all, True),
-        gather_columns(lines, me, small, small_all, False),
-        gather_columns(lines, me, small, small_all, True),
-    )
-    wait_all(waits)
+        *[(0, gather_columns(lines, me, small, small_all, (other, 0, 128))) for other in (False, True)],
+        *[(at, work) for at, work in enumerate(works)],
+        *[
+            (at, gather_rows(lines, me, out, out_all, *piece))
+            for at, piece in enumerate(row_pieces(out.shape[0], OUT_PARTS))
+        ],
+        (1, gather_team(lines, me, tokens, tokens_all, 3)),
+    )
     lines.finish()
 
 
 def middle_kernel(
-    zhs, tokens, partial, upstream, gate_cut, up_cut, down, gain, bias,
-    middle, input_all, upstream_all, gate_all, up_all, down_all,
-    own, taken, second, send, recv, local,
+    zhs, tokens, upstream, tokens_all, qkv_all, out_all, gate_cut, up_cut, down,
+    first_gain, first_bias, offset, gain, bias, tables,
+    middle, first_out, queries_out, keys_out, values_out, mixed_out,
+    upstream_all, input_all, gate_all, up_all, down_all,
+    whole, first, weight, out_weight, queries, keys, values, mixed, partial,
+    own, passed, taken, second, send, recv, local,
 ):
     me, lines = Place(zhs), Lines(send, recv, local)
+    loads = [lines.copy(tokens_all, whole), lines.copy(qkv_all, weight), lines.copy(out_all, out_weight)]
     me.greet()
-    waits = sum_team(lines, me, partial, own, taken)
-    late = []
+    spawned = []
 
     def tokens_work():
+        loads[0]()
+
+        def normed(rows):
+            first[rows] = (norm_rows(whole[rows].astype(F32))[0] * first_gain[...] + first_bias[...]).astype(BF)
+
+        by_rows(whole.shape[0], normed)
+        loads[1]()
         yield
-        wait_all(waits)
+        yield from forward_attention(first, weight, offset, tables, queries, keys, values, mixed)
+        loads[2]()
+        for start in range(0, partial.shape[3], 512):
+            block = dot(mixed[...], out_weight[:, start : start + 512])
+            partial[:, :, :, start : start + 512] = block.astype(BF).reshape(partial.shape[:3] + (512,))
+        yield from sum_team(lines, me, partial, own, passed, taken, 2)
 
         def body(rows):
             values = tokens[rows].astype(F32) + team_total(own, taken, rows)
@@ -494,35 +656,58 @@
             second[rows] = (norm_rows(values)[0] * gain[...] + bias[...]).astype(BF)
 
         by_rows(middle.shape[0], body)
-        late.extend(gather_team(lines, me, second, input_all))
-        late.extend(gather_team(lines, me, upstream, upstream_all))
-
+        kept = [
+            lines.copy(source, target)
+            for source, target in (
+                (first, first_out), (queries, queries_out), (keys, keys_out), (values, values_out), (mixed, mixed_out),
+            )
+        ]
+        yield from gather_team(lines, me, second, input_all, 3)
+        wait_all(kept)
+
+    rows = [gather_rows(lines, me, down, down_all, *piece) for piece in row_pieces(down.shape[0], DOWN_PARTS)]
+    columns = [
+        gather_columns(lines, me, cut, found, piece)
+        for piece in column_pieces(gate_cut.shape[2], FF_PARTS)
+        for cut, found in ((gate_cut, gate_all), (up_cut, up_all))
+    ]
     run(
-        *[gather_rows(lines, me, down, down_all, start, size) for start, size in halves(down.shape[0])],
-        gather_columns(lines, me, gate_cut, gate_all, False),
-        gather_columns(lines, me, up_cut, up_all, False),
-        tokens_work(),
-        gather_columns(lines, me, gate_cut, gate_all, True),
-        gather_columns(lines, me, up_cut, up_all, True),
-    )
-    wait_all(late)
+        *enumerate(rows),
+        (0, tokens_work()),
+        *[(max(0, len(rows) + at - 1), work) for at, work in enumerate(columns)],
+        (1, gather_team(lines, me, upstream, upstream_all, 4)),
+    )
     lines.finish()
 
 
 def back_kernel(
     zhs, middle, upstream, gain, partial_down, partial_second, grad_down, grad_gate, grad_up,
-    result, grad_middle, sums, attended_all, down_total, gate_cut, up_cut,
-    own_down, taken_down, own_second, taken_second, attended, buffers, send, recv, local,
+    out_all, queries_in, keys_in, values_in, mixed_in, tables,
+    result, grad_middle, sums, down_total, gate_cut, up_cut, out_total, projected_out, bias_sums,
+    own_down, passed_down, taken_down, own_second, passed_second, taken_second, attended,
+    attended_all, out_weight, queries, keys, values, mixed, grad_mixed, grad_projected, grad_out,
+    buffers, send, recv, local,
 ):
     me, lines = Place(zhs), Lines(send, recv, local)
+    loads = [
+        lines.copy(source, target)
+        for source, target in (
+            (out_all, out_weight), (queries_in, queries), (keys_in, keys), (values_in, values), (mixed_in, mixed),
+        )
+    ]
     me.greet()
-    waits = sum_team(lines, me, partial_second, own_second, taken_second)
-    late = []
+    spawned = []
+    pieces = column_pieces(gate_cut.shape[2], FF_PARTS)
+    works = [
+        sum_rows(lines, me, grad_down, down_total, buffers[at], piece[0])
+        for at, piece in enumerate(row_pieces(down_total.shape[0], DOWN_PARTS))
+    ]
+    for piece in pieces:
+        for grad, cut in ((grad_gate, gate_cut), (grad_up, up_cut)):
+            works.append(sum_columns(lines, me, grad, cut, buffers[len(works)], piece))
 
     def tokens_work():
-        yield
-        wait_all(waits)
-        late.extend(sum_team(lines, me, partial_down, own_down, taken_down))
+        yield from sum_team(lines, me, partial_second, own_second, passed_second, taken_second, 2)
         sums[...] = jnp.zeros_like(sums)
 
         def body(rows):
@@ -535,45 +720,60 @@
             attended[rows] = grad.astype(BF)
 
         by_rows(middle.shape[0], body)
-        shared = gather_team(lines, me, attended, attended_all)
+        yield from gather_team(lines, me, attended, attended_all, 2)
+        wait_all(loads)
+        count, width = mixed.shape[0], attended_all.shape[3]
+        for start in range(0, width, 512):
+            block = dot_tn(mixed[...], attended_all[:, :, :, start : start + 512].reshape(count, 512))
+            grad_out[:, :, :, :, start : start + 512] = block.astype(BF).reshape(grad_out.shape[:4] + (512,))
+        for at, piece in enumerate(row_pieces(out_total.shape[0], OUT_PARTS)):
+            spawned.append(sum_rows(lines, me, grad_out, out_total, buffers[len(works) + at], piece[0]))
+        grad_mixed[...] = dot_nt(attended_all[...].reshape(count, width), out_weight[...]).astype(BF)
         yield
-        wait_all(late)
-
-        def last(rows):
+        yield from backward_attention(grad_mixed, tables, queries, keys, values, grad_projected)
+        wait = lines.copy(grad_projected, projected_out)
+        for start in range(0, grad_projected.shape[1], 256):
+            block = jnp.sum(grad_projected[:, start : start + 256].astype(F32), axis=0, keepdims=True)
+            bias_sums[:, start : start + 256] = block
+        yield
+        wait()
+
+    def result_work():
+        yield from sum_team(lines, me, partial_down, own_down, passed_down, taken_down, 3)
+
+        def body(rows):
             result[rows] = (middle[rows] + team_total(own_down, taken_down, rows)).astype(BF)
 
-        by_rows(middle.shape[0], last)
-        yield
-        wait_all(shared)
-
-    pieces = halves(down_total.shape[0])
-    run(
-        *[
-            sum_rows(lines, me, grad_down, down_total, buffers[at], start)
-            for at, (start, size) in enumerate(pieces)
-        ],
-        tokens_work(),
-        sum_columns(lines, me, grad_gate, gate_cut, buffers[len(pieces)], False),
-        sum_columns(lines, me, grad_up, up_cut, buffers[len(pieces) + 1], False),
-        sum_columns(lines, me, grad_gate, gate_cut, buffers[len(pieces) + 2], True),
-        sum_columns(lines, me, grad_up, up_cut, buffers[len(pieces) + 3], True),
-    )
+        by_rows(middle.shape[0], body)
+
+    run(*enumerate(works), (0, tokens_work()), (7, result_work()), spawned=spawned)
     lines.finish()
 
 
 def leave_kernel(
-    zhs, tokens, grad_middle, gain, partial, vector, grad_out, grad_qkv,
-    grad_inputs, sums, out_total, qkv_cut,
-    own, taken, steps, buffers, send, recv, local,
+    zhs, tokens, grad_middle, gain, second_sums, bias_sums, grad_projected, first_in, qkv_in,
+    grad_inputs, sums, qkv_cut,
+    first, weight, partial, grad_qkv, own, passed, taken, steps, buffers, send, recv, local,
 ):
     me, lines = Place(zhs), Lines(send, recv, local)
+    loads = [lines.copy(first_in, first), lines.copy(qkv_in, weight)]
     me.greet()
-    waits = sum_team(lines, me, partial, own, taken)
 
     def tokens_work():
-        yield
-        wait_all(waits)
-        steps[0] = vector[...]
+        for at in range(weight.shape[0] // 256):
+            block = dot_nt(grad_projected[...], weight[at * 256 : at * 256 + 256])
+            partial[:, :, :, at * 256 : at * 256 + 256] = block.astype(BF).reshape(partial.shape[:3] + (256,))
+        yield from sum_team(lines, me, partial, own, passed, taken, 2)
+        steps[0] = jnp.zeros_like(steps[0])
+        steps[0, 2:4] = second_sums[0:2]
+        part = bias_sums.shape[1] // 3
+        block = part // zhs
+        for number in range(3):
+            for zh in range(zhs):
+                at = ((me.s * zhs + zh) * 2 + me.zl) * block
+                steps[0, 4 + number : 5 + number, pl.ds(pl.multiple_of(at, 64), block)] = bias_sums[
+                    :, number * part + zh * block : number * part + (zh + 1) * block
+                ]
 
         def body(rows):
             normed, scale_rows = norm_rows(tokens[rows].astype(F32))
@@ -602,16 +802,19 @@
             steps[at] = total
         sums[...] = steps[at]
 
-    pieces = halves(out_total.shape[0])
-    run(
-        *[
-            sum_rows(lines, me, grad_out, out_total, buffers[at], start)
-            for at, (start, size) in enumerate(pieces)
-        ],
-        tokens_work(),
-        sum_columns(lines, me, grad_qkv, qkv_cut, buffers[len(pieces)], False),
-        sum_columns(lines, me, grad_qkv, qkv_cut, buffers[len(pieces) + 1], True),
-    )
+    wait_all(loads)
+    at = 0
+    for s in range(grad_qkv.shape[0]):
+        for zh in range(zhs):
+            for zl in range(grad_qkv.shape[2]):
+                block = dot_tn(first[:, at : at + 4 * grad_qkv.shape[5]], grad_projected[...])
+                grad_qkv[s, zh, zl] = block.astype(BF).reshape(grad_qkv.shape[3:])
+                at += 4 * grad_qkv.shape[5]
+    works = [
+        sum_columns(lines, me, grad_qkv, qkv_cut, buffers[at], piece)
+        for at, piece in enumerate(column_pieces(qkv_cut.shape[2], QKV_PARTS))
+    ]
+    run(*enumerate(works), (1, tokens_work()))
     lines.finish()
 
 
@@ -694,6 +897,9 @@
     small = jnp.broadcast_to(small, (team, 8, 128))
     token_shape = (seqs, half, rows, width)
     owners = (half, zh, seqs, 2, 2)
+    count = team * rows
+    limit = 56
+    tables = rotary_tables(length)
     tokens_all, small_all, qkv_all, out_all = call(
         enter_kernel, zh, 0,
         [(tokens, IN_HBM), (small, IN_HBM), (cut_columns(qkv_weight, 3), IN_HBM), (out_weight, IN_HBM)],
@@ -703,62 +909,51 @@
             (owners + (own, 3 * part), BF, IN_HBM),
             ((zh, 2, 2, own, width), BF, IN_HBM),
         ],
-        [], 12 + 5 * (zh + 4), 8, 16,
+        [], 3 + (2 + OUT_PARTS + 2 * QKV_PARTS) * (zh + 4), 24, 16,
     )
     small = small_all.reshape(devices, 1024)
     first_gain = small[:, :own].reshape(1, width)
     first_bias = small[:, own : 2 * own].reshape(1, width)
     second_gain = small[:, 2 * own : 3 * own].reshape(1, width)
     second_bias = small[:, 3 * own : 4 * own].reshape(1, width)
-    qkv_offset = mine_columns(small[:, 4 * own : 7 * own].reshape(-1), 3)
+    qkv_offset = mine_columns(small[:, 4 * own : 7 * own].reshape(-1), 3).reshape(1, 3 * part)
     qkv_matrix = qkv_all.reshape(width, 3 * part)
     out_matrix = out_all.reshape(part, width)
 
-    first_input = (
-        norm_rows(tokens_all.reshape(-1, width).astype(F32))[0] * first_gain + first_bias
-    ).astype(BF)
-    projected = dot(first_input, qkv_matrix) + qkv_offset
-    group_heads = part // HEAD_DIM
-    positions = jnp.tile(jnp.arange(length, dtype=jnp.int32), seqs)
-
-    def heads_of(values):
-        return values.reshape(seqs, length, group_heads, HEAD_DIM).transpose(0, 2, 1, 3)
-
-    def unheads(values):
-        return values.transpose(0, 2, 1, 3).reshape(seqs * length, part)
-
-    queries = heads_of(rotate(projected[:, :part].reshape(-1, group_heads, HEAD_DIM), positions, 1.0).astype(BF))
-    keys = heads_of(rotate(projected[:, part : 2 * part].reshape(-1, group_heads, HEAD_DIM), positions, 1.0).astype(BF))
-    values = heads_of(projected[:, 2 * part :].astype(BF))
-    causal = jnp.arange(length)[:, None] >= jnp.arange(length)[None, :]
-    scores = jnp.einsum("shqd,shkd->shqk", queries, keys, preferred_element_type=F32) * 0.125
-    scores = jnp.where(causal, scores, -1e30)
-    highest = jnp.max(scores, axis=-1, keepdims=True)
-    exponent = jnp.exp(scores - highest)
-    probs = exponent / jnp.sum(exponent, axis=-1, keepdims=True)
-    probs_low = probs.astype(BF)
-    mixed = unheads(jnp.einsum("shqk,shkd->shqd", probs_low, values, preferred_element_type=F32).astype(BF))
-    partial = dot(mixed, out_matrix).astype(BF).reshape(token_shape)
-
-    limit = 48
-    token_scratch = [pltpu.VMEM((rows, width), BF), pltpu.VMEM((3, rows, width), BF)]
-    middle, input_all, upstream_all, gate_all, up_all, down_all = call(
+    token_scratch = [
+        pltpu.VMEM((rows, width), BF), pltpu.VMEM((rows, width), BF), pltpu.VMEM((3, rows, width), BF)
+    ]
+    head_shape = (count, part)
+    heads = [(head_shape, BF, IN_HBM)] * 4
+    head_scratch = [pltpu.VMEM(head_shape, BF)] * 4
+    (
+        middle, first_input, queries, keys, values, mixed, upstream_all, input_all, gate_all, up_all, down_all,
+    ) = call(
         middle_kernel, zh, 1,
         [
-            (tokens, IN_VMEM), (partial, IN_HBM), (cotangent, IN_HBM),
-            (cut_columns(gate_weight, 1), IN_HBM), (cut_columns(up_weight, 1), IN_HBM),
-            (down_weight, IN_HBM), (second_gain, IN_VMEM), (second_bias, IN_VMEM),
+            (tokens, IN_VMEM), (cotangent, IN_HBM), (tokens_all.reshape(count, width), IN_HBM),
+            (qkv_matrix, IN_HBM), (out_matrix, IN_HBM),
+            (cut_columns(gate_weight, 1), IN_HBM), (cut_columns(up_weight, 1), IN_HBM), (down_weight, IN_HBM),
+            (first_gain, IN_VMEM), (first_bias, IN_VMEM), (qkv_offset, IN_VMEM),
+            (second_gain, IN_VMEM), (second_bias, IN_VMEM), (tables, IN_VMEM),
         ],
         [
             ((rows, width), F32, IN_VMEM),
+            ((count, width), BF, IN_HBM),
+            *heads,
             (token_shape, BF, IN_HBM),
             (token_shape, BF, IN_HBM),
             (owners + (own, ff_part), BF, IN_HBM),
             (owners + (own, ff_part), BF, IN_HBM),
             ((zh, 2, 2, ff_own, width), BF, IN_HBM),
         ],
-        [*token_scratch, pltpu.VMEM((rows, width), BF)],
-        9 + 6 * (zh + 4), 16, limit,
+        [
+            pltpu.VMEM((count, width), BF), pltpu.VMEM((count, width), BF),
+            pltpu.VMEM((width, 3 * part), BF), pltpu.VMEM((part, width), BF),
+            *head_scratch, pltpu.VMEM(token_shape, BF),
+            *token_scratch, pltpu.VMEM((rows, width), BF),
+        ],
+        9 + (DOWN_PARTS + 4 * FF_PARTS) * (zh + 4), 40, limit,
     )
     second_input = input_all.reshape(-1, width)
     upstream = upstream_all.reshape(-1, width)
@@ -777,75 +972,60 @@
     grad_gate = (grad_hidden * up_rows * sigmoid_gate * (1.0 + gate_rows * (1.0 - sigmoid_gate))).astype(BF)
     grad_up = (grad_hidden * silu_gate).astype(BF)
     partial_second = (dot_nt(grad_gate, gate_matrix) + dot_nt(grad_up, up_matrix)).astype(BF).reshape(token_shape)
-    pieces = [size for _, size in halves(ff_own)]
-    result, grad_middle, second_sums, attended_all, down_total, gate_cut, up_cut = call(
+    result, grad_middle, second_sums, down_total, gate_cut, up_cut, out_total, grad_projected, bias_sums = call(
         back_kernel, zh, 2,
         [
             (middle, IN_VMEM), (cotangent, IN_VMEM), (second_gain, IN_VMEM),
             (partial_down, IN_HBM), (partial_second, IN_HBM), (grad_down, IN_HBM),
             (dot_tn(second_input, grad_gate).astype(BF).reshape(gate_all.shape), IN_HBM),
             (dot_tn(second_input, grad_up).astype(BF).reshape(up_all.shape), IN_HBM),
+            (out_matrix, IN_HBM), (queries, IN_HBM), (keys, IN_HBM), (values, IN_HBM), (mixed, IN_HBM),
+            (tables, IN_VMEM),
         ],
         [
             ((rows, width), BF, IN_VMEM),
             ((rows, width), F32, IN_VMEM),
             ((8, width), F32, IN_VMEM),
-            (token_shape, BF, IN_HBM),
             ((ff_own, width), F32, IN_HBM),
             ((team, own, ff_part), BF, IN_HBM),
             ((team, own, ff_part), BF, IN_HBM),
-        ],
-        [
-            *token_scratch, *token_scratch, pltpu.VMEM((rows, width), BF),
-            [row_buffers(zh, size, width) for size in pieces]
-            + [column_buffers(zh, own, ff_part) for _ in range(4)],
-        ],
-        9 + 6 * (zh + 4), 20, limit,
-    )
-
-    grad_attended = attended_all.reshape(-1, width)
-    grad_out = dot_tn(mixed, grad_attended).astype(BF).reshape(out_all.shape)
-    grad_mixed = heads_of(dot_nt(grad_attended, out_matrix).astype(BF))
-    grad_probs = jnp.einsum("shqd,shkd->shqk", grad_mixed, values, preferred_element_type=F32)
-    grad_scores = (probs * (grad_probs - jnp.sum(probs * grad_probs, axis=-1, keepdims=True))).astype(BF)
-    grad_queries = (jnp.einsum("shqk,shkd->shqd", grad_scores, keys, preferred_element_type=F32) * 0.125).astype(BF)
-    grad_keys = (jnp.einsum("shqk,shqd->shkd", grad_scores, queries, preferred_element_type=F32) * 0.125).astype(BF)
-    grad_values = jnp.einsum("shqk,shqd->shkd", probs_low, grad_mixed, preferred_element_type=F32).astype(BF)
-    grad_queries = rotate(unheads(grad_queries).astype(F32).reshape(-1, group_heads, HEAD_DIM), positions, -1.0)
-    grad_keys = rotate(unheads(grad_keys).astype(F32).reshape(-1, group_heads, HEAD_DIM), positions, -1.0)
-    grad_projected = jnp.concatenate(
-        [grad_queries.reshape(-1, part).astype(BF), grad_keys.reshape(-1, part).astype(BF), unheads(grad_values)],
-        axis=1,
-    )
-    partial_first = dot_nt(grad_projected, qkv_matrix).astype(BF).reshape(token_shape)
-    bias_part = jnp.sum(grad_projected.astype(F32), axis=0).reshape(3, zh, -1)
-    bias_whole = jnp.zeros((3, half, zh, seqs, bias_part.shape[2]), F32)
-    bias_whole = lax.dynamic_update_slice(
-        bias_whole, bias_part[:, None, :, None], (0, lax.axis_index("seq"), 0, lax.axis_index("zl"), 0)
-    ).reshape(3, width)
-    vector = jnp.concatenate(
-        [jnp.zeros((2, width), F32), second_sums[:2], bias_whole, jnp.zeros((1, width), F32)], axis=0
-    )
-    pieces = [size for _, size in halves(own)]
-    grad_inputs, sums, out_total, qkv_cut = call(
+            ((own, width), F32, IN_HBM),
+            ((count, 3 * part), BF, IN_HBM),
+            ((1, 3 * part), F32, IN_VMEM),
+        ],
+        [
+            *token_scratch, *token_scratch, pltpu.VMEM((rows, width), BF), pltpu.VMEM(token_shape, BF),
+            pltpu.VMEM((part, width), BF), *head_scratch, pltpu.VMEM(head_shape, BF),
+            pltpu.VMEM((count, 3 * part), BF), pltpu.VMEM(out_all.shape, BF),
+            [row_buffers(zh, size, width) for _, size in row_pieces(ff_own, DOWN_PARTS)]
+            + [
+                column_buffers(zh, own, size)
+                for _, _, size in column_pieces(ff_part, FF_PARTS)
+                for _ in range(2)
+            ]
+            + [row_buffers(zh, size, width) for _, size in row_pieces(own, OUT_PARTS)],
+        ],
+        9 + (OUT_PARTS + DOWN_PARTS + 4 * FF_PARTS) * (zh + 4), 50, 60,
+    )
+    grad_inputs, sums, qkv_cut = call(
         leave_kernel, zh, 3,
         [
             (tokens, IN_VMEM), (grad_middle, IN_VMEM), (first_gain, IN_VMEM),
-            (partial_first, IN_HBM), (vector, IN_VMEM), (grad_out, IN_HBM),
-            (dot_tn(first_input, grad_projected).astype(BF).reshape(qkv_all.shape), IN_HBM),
+            (second_sums, IN_VMEM), (bias_sums, IN_VMEM), (grad_projected, IN_VMEM),
+            (first_input, IN_HBM), (qkv_matrix, IN_HBM),
         ],
         [
             ((rows, width), F32, IN_VMEM),
             ((8, width), F32, IN_VMEM),
-            ((own, width), F32, IN_HBM),
             ((team, own, 3 * part), BF, IN_HBM),
         ],
         [
+            pltpu.VMEM((count, width), BF), pltpu.VMEM((width, 3 * part), BF), pltpu.VMEM(token_shape, BF),
+            pltpu.VMEM(qkv_all.shape, BF),
             *token_scratch, pltpu.VMEM((zh + 9, 8, width), F32),
-            [row_buffers(zh, size, width) for size in pieces]
-            + [column_buffers(zh, own, 3 * part) for _ in range(2)],
-        ],
-        3 + zh + 3 + 4 * (zh + 4), 12, limit,
+            [column_buffers(zh, own, size) for _, _, size in column_pieces(3 * part, QKV_PARTS)],
+        ],
+        zh + 6 + (2 * QKV_PARTS) * (zh + 4), 24, limit,
     )
 
     def mine(vector_row, size):

time: 802 us -> 628 us (0.78)
  matrix products: 137 us -> 63.4 us
  local copies, waits for them, and re-layouts: 93.9 us -> 52.1 us
  Pallas kernels: 545 us -> 504 us
  other arithmetic: 15.3 us -> 0.01 us
    pallas_call x4, Pallas kernels: 545 us -> 504 us  [call(): pl.pallas_call(lambda *refs: kernel(zhs, *refs), out_shape=[jax.ShapeDtyp...]
    dot_general x5 -> x0, matrix products: 20 us -> none  [the longest x1 7.95 us: per_device(): jnp.einsum('shqd,shkd->shqk', grad_mixed, values, preferred_element_type=...]
    dot_general x5 -> x3, matrix products: 39.1 us -> 20.3 us  [dot_nt(): lax.dot_general(left, right, (((1,), (1,)), ((), ())), preferred_element_...]
    dot_general x5 -> x3, matrix products: 35.2 us -> 20.4 us  [dot_tn(): lax.dot_general(left, right, (((0,), (0,)), ((), ())), preferred_element_...]
    dot_general x5 -> x3, matrix products: 35.7 us -> 22.7 us  [dot(): return jnp.dot(left, right, preferred_element_type=F32)]
    convert_element_type x8 -> x0, local copies, waits for them, and re-layouts: 12.2 us -> none  [the longest x2 5.27 us: per_device(): unheads(grad_keys).astype(F32).reshape(-1, group_heads, HEAD_DIM)]
    reshape x6 -> x1, local copies, waits for them, and re-layouts: 12.2 us -> 0.68 us  [per_device(): first_bias = small[:, own:2 * own].reshape(1, width)]
    convert_element_type x6 -> x0, other arithmetic: 10.8 us -> none  [the longest x1 7.1 us: per_device(): (probs * (grad_probs - jnp.sum(probs * grad_probs, axis=-1, keepdims=True...]
where the time goes in v3:
time: 628 us; the launch traced here: 621 us
  Pallas kernels  504 us (80%)
  matrix products  63.4 us (10%)
  local copies, waits for them, and re-layouts  52.1 us (8%)
    pallas_call x4, Pallas kernels, call(): pl.pallas_call(lambda *refs: kernel(zhs, *refs), out_shape=[jax.ShapeDtyp...  504 us
    dot_general x3, matrix products, dot(): return jnp.dot(left, right, preferred_element_type=F32)  22.7 us
    dot_general x3, matrix products, dot_tn(): lax.dot_general(left, right, (((0,), (0,)), ((), ())), preferred_element_...  20.4 us
    dot_general x3, matrix products, dot_nt(): lax.dot_general(left, right, (((1,), (1,)), ((), ())), preferred_element_...  20.3 us
    convert_element_type x9, local copies, waits for them, and re-layouts, join_columns(): return cut.reshape(own, -1).astype(F32)  19.3 us

profile of v3, /device:TPU:0, one launch (start us, length us, event | category | flops | bytes accessed | tf_op | source)
XLA Modules:
  0.0 621.0 jit_solution(1823731594905696174)
XLA Ops:
  0.6 0.0 copy-start.7
  0.7 3.5 concatenate.3
  4.2 2.6 reshape.132
  6.8 0.6 copy.40
  7.4 0.5 reshape.133.refs_2_
  7.9 0.0 copy-done.7
  7.9 0.9 reshape.137
  8.8 0.6 copy.39
  9.4 1.4 reshape.138.refs_5_
  10.8 2.9 reshape.139
  13.7 0.6 copy.38
  14.3 1.4 reshape.140.refs_6_
  15.7 0.0 copy-done.2
  15.7 0.0 copy-done.4
  15.7 76.8 %shard_map.220 = (bf16[2,2,160,2048]{3,2,1,0:T(8,128)(2,1)S(1)}, f32[2,2,2,2,2,8,128]{6,5,4,3,2,1,0:T(8,128)S(1)}, bf16[2,2,2,2,2,64,1536]{6,5,4,3,2,1,0:T(8,128)(2,1)S(1)}, bf16[2,2,2,64,2048]{4,3,2,1,0:T(8,128)(2,1)S(1)}) custom-call(bf16[160,2048]{1,0:T(8,128)(2,1)S(1)} %bitcast.78, f32[4,8,128]{2,1,0:T(8,128)S(1)} %broadcast_in_dim.9.refs_1_, ...), custom_call_target="tpu_custom_call" | custom-call | tf_op jit(solution)/shard_map/pallas_call | solution.py:839
  92.5 0.0 copy-start
  92.5 2.6 copy-done
  95.2 1.3 copy-done.1
  96.5 1.5 copy-done.3
  98.0 0.1 fusion.5
  98.1 0.1 reshape_reshape.6
  98.2 0.6 constant_dynamic-slice_fusion.4
  98.8 0.7 reshape.145.refs_12_
  99.5 0.7 reshape.144.refs_11_.refs_2_
  100.1 0.7 reshape.142.refs_8_.refs_2_
  100.8 0.7 reshape.143.refs_9_
  101.5 180.0 %shard_map.221 = (f32[160,2048]{1,0:T(8,128)}, bf16[640,2048]{1,0:T(8,128)(2,1)}, bf16[640,512]{1,0:T(8,128)(2,1)}, bf16[640,512]{1,0:T(8,128)(2,1)}, bf16[640,5...) custom-call(bf16[160,2048]{1,0:T(8,128)(2,1)} %bitcast.76, ...), custom_call_target="tpu_custom_call" | custom-call | tf_op jit(solution)/shard_map/pallas_call | solution.py:839
  281.5 0.0 copy-start.9
  281.5 0.0 copy-start.10
  281.5 0.0 slice-start.2
  281.5 9.6 %fusion.8 = f32[640,1408]{1,0:T(8,128)} fusion(bf16[640,2048]{1,0:T(8,128)(2,1)} %bitcast.109, bf16[2048,1408]{1,0:T(8,128)(2,1)} %bitcast.99), kind=kOutput, calls=%fused_computation.27 | convolution fusion | flops 3690987520 | bytes 11993088 | tf_op jit(solution)/shard_map/dot_general | solution.py:54
  291.1 0.0 copy-done.9
  291.1 0.0 slice-start
  291.1 6.0 fusion.7
  297.2 10.5 %multiply_convert_fusion = (bf16[640,1408]{1,0:T(8,128)(2,1)}, bf16[640,1408]{1,0:T(8,128)(2,1)S(1)}, bf16[640,1408]{1,0:T(8,128)(2,1)}) fusion(f32[640,1408]{1,0:T(8,128)} %fusion.7, f32[640,1408]{1,0:T(8,128)} %fusion.8, bf16[640,2048]{1,0:T(8,128)(2,1)} %bitcast.113, bf16[1408,2048]{1,0:T(8,128)(2,1)S(1)} %bitcast.107), kind=kOutput, calls=%fused_computation.4 | convolution fusion | flops 3704504320 | bytes 21004288 | tf_op jit(solution)/shard_map/dot_general | solution.py:58
  307.6 7.1 %convolution_convert_fusion.3 = bf16[640,2048]{1,0:T(8,128)(2,1)} fusion(bf16[640,1408]{1,0:T(8,128)(2,1)} %get-tuple-element.68, bf16[1408,2048]{1,0:T(8,128)(2,1)S(1)} %bitcast.108), kind=kOutput, calls=%fused_computation.9 | convolution fusion | flops 3692298240 | bytes 10190848 | tf_op jit(solution)/shard_map/dot_general | solution.py:54
  314.7 4.2 fusion.9
  319.0 5.6 add_convert_fusion
  324.7 0.0 copy-done.14
  324.7 6.5 %convolution_convert_fusion.2 = bf16[1408,2048]{1,0:T(8,128)(2,1)} fusion(bf16[640,1408]{1,0:T(8,128)(2,1)S(1)} %copy-done.14, bf16[640,2048]{1,0:T(8,128)(2,1)S(1)} %bitcast.114), kind=kOutput, calls=%fused_computation.2 | convolution fusion | flops 3693871104 | bytes 10190848 | tf_op jit(solution)/shard_map/dot_general | solution.py:62
  331.2 7.0 %convolution_convert_fusion = bf16[2048,1408]{1,0:T(8,128)(2,1)} fusion(bf16[640,2048]{1,0:T(8,128)(2,1)S(1)} %bitcast.111, bf16[640,1408]{1,0:T(8,128)(2,1)S(1)} %copy-done.13), kind=kOutput, calls=%fused_computation | convolution fusion | flops 3693871104 | bytes 10190848 | tf_op jit(solution)/shard_map/dot_general | solution.py:62
  338.2 6.8 %convolution_convert_fusion.1 = bf16[2048,1408]{1,0:T(8,128)(2,1)} fusion(bf16[640,2048]{1,0:T(8,128)(2,1)S(1)} %bitcast.112, bf16[640,1408]{1,0:T(8,128)(2,1)S(1)} %get-tuple-element.67), kind=kOutput, calls=%fused_computation.1 | convolution fusion | flops 3693871104 | bytes 10190848 | tf_op jit(solution)/shard_map/dot_general | solution.py:62
  345.1 163.8 %shard_map.222 = (bf16[160,2048]{1,0:T(8,128)(2,1)}, f32[160,2048]{1,0:T(8,128)}, f32[8,2048]{1,0:T(8,128)}, f32[176,2048]{1,0:T(8,128)}, bf16[4,64,1408]{2,1,0:...) custom-call(f32[160,2048]{1,0:T(8,128)} %get-tuple-element.43.refs_0, ...), custom_call_target="tpu_custom_call" | custom-call | tf_op jit(solution)/shard_map/pallas_call | solution.py:839
  508.9 83.5 %shard_map.223 = (f32[160,2048]{1,0:T(8,128)}, f32[8,2048]{1,0:T(8,128)}, bf16[4,64,1536]{2,1,0:T(8,128)(2,1)}) custom-call(bf16[160,2048]{1,0:T(8,128)(2,1)} %bitcast.77, f32[160,2048]{1,0:T(8,128)} %get-tuple-element.54.refs_1_, f32[1,2048]{1,0:T(1,128)} %reshape.142.refs_8_.refs_2_, f32[8,2048]{1,0:T(8,128)} %get-tuple-element.55.refs_3_, ...), custom_call_target="tpu_custom_call" | custom-call | tf_op jit(solution)/shard_map/pallas_call | solution.py:839
  592.4 0.8 slice.37
  593.3 1.0 fusion.6
  594.3 0.6 dynamic_slice.34
  595.0 0.6 fusion.3
  595.5 0.6 fusion.1
  596.1 2.5 reshape.162
  598.6 1.2 copy.29
  599.8 2.4 reshape.159
  602.2 2.6 reshape.163
  604.8 1.2 copy.30
  606.1 2.8 reshape.160
  608.9 2.6 reshape.164
  611.5 1.2 copy.31
  612.7 0.0 copy-start.6
  612.7 2.8 reshape.161
  615.5 2.1 copy.46
  617.6 1.1 copy.47
  618.7 0.0 copy-done.8
  618.7 0.8 copy.48
  619.5 1.1 copy.49
  (29 shorter events, 0.1 us)
Async XLA Ops:
  0.6 7.2 %copy-start.7 = (bf16[64,5632]{1,0:T(8,128)(2,1)S(1)}, bf16[64,5632]{1,0:T(8,128)(2,1)}, u32[]{:S(2)}) copy-start(bf16[64,5632]{1,0:T(8,128)(2,1)} %param.22) | copy-start | bytes 2162692
  10.8 4.9 copy-start.2
  10.8 4.9 copy-start.4
  92.5 2.6 copy-start
  95.2 1.3 copy-start.1
  96.5 1.5 copy-start.3
  281.5 9.6 %copy-start.9 = (bf16[2,2,2,2,2,64,1408]{6,5,4,3,2,1,0:T(8,128)(2,1)S(1)}, bf16[2,2,2,2,2,64,1408]{6,5,4,3,2,1,0:T(8,128)(2,1)}, u32[]{:S(2)}) copy-start(bf16[2,2,2,2,2,64,1408]{6,5,4,3,2,1,0:T(8,128)(2,1)} %get-tuple-element.45) | copy-start | bytes 17301508
  281.5 9.6 %copy-start.10 = (bf16[2,2,160,2048]{3,2,1,0:T(8,128)(2,1)S(1)}, bf16[2,2,160,2048]{3,2,1,0:T(8,128)(2,1)}, u32[]{:S(2)}) copy-start(bf16[2,2,160,2048]{3,2,1,0:T(8,128)(2,1)} %get-tuple-element.44) | copy-start | bytes 7864324
  281.5 15.6 %slice-start.2 = ((s8[5767168]{0:T(1024)(128)(4,1)}), s8[4194304]{0:T(1024)(128)(4,1)S(1)}, s32[]{:S(2)}) async-start(s8[5767168]{0:T(1024)(128)(4,1)} %bitcast.105), calls=%async_computation.2 | async-start | bytes 8388608
  291.1 6.0 slice-start.3
  291.1 27.9 %slice-start = ((s8[5767168]{0:T(1024)(128)(4,1)}), s8[4194304]{0:T(1024)(128)(4,1)S(1)}, s32[]{:S(2)}) async-start(s8[5767168]{0:T(1024)(128)(4,1)} %bitcast.100), calls=%async_computation | async-start | bytes 8388608
  297.2 21.8 %slice-start.1 = ((s8[5767168]{0:T(1024)(128)(4,1)}), s8[1572864]{0:T(1024)(128)(4,1)S(1)}, s32[]{:S(2)}) async-start(s8[5767168]{0:T(1024)(128)(4,1)} %bitcast.100), calls=%async_computation.1 | async-start | bytes 3145728
  314.7 4.3 copy-start.13
  319.0 5.6 copy-start.12
  319.0 5.6 copy-start.14
  324.7 6.5 %copy-start.11 = (bf16[2,2,160,2048]{3,2,1,0:T(8,128)(2,1)S(1)}, bf16[2,2,160,2048]{3,2,1,0:T(8,128)(2,1)}, u32[]{:S(2)}) copy-start(bf16[2,2,160,2048]{3,2,1,0:T(8,128)(2,1)} %get-tuple-element.44) | copy-start | bytes 7864324
  612.7 4.9 copy-start.6
  615.5 3.2 copy-start.8
  615.5 4.0 copy-start.5
